TPU v7x, 32 devices: a whole 2x2x4 slice. The times are simulated.
32 devices in a mesh: row: 8 (over z, x), col: 4 (over y, core).
Axes of the slice: x: 2, y: 2, z: 4, core: 2. Of those that a mesh axis runs over, the one named last changes fastest.
Arguments:
- elemental: bfloat16 [2, 512, 512, 512], P(None, 'row', 'col'), may hold values from -6 to 6
- perambulators: bfloat16 [32, 2, 512, 512], P(('row', 'col')), may hold values from -0.1875 to 0.1875
- source_owner: int32 [1], replicated, may hold values from 0 to 31
Outputs:
- contracted: float32 [2, 512, 512, 512], P(None, None, 'row', 'col')
All inputs are finite; a program needn't handle non-finite values.
Results may differ from a plain program's by a relative error of at most 0.0041.
Values may be sent and summed in bfloat16 or wider, within the bound.
No kernel may reach another device: no remote copies, remote signals or barrier semaphores. Data moves between devices by JAX's collectives and lax.ppermute only.
A program may use at most 128 MiB of HBM per device.

v0:
```python
import jax
import jax.numpy as jnp
from jax import lax
from jax.sharding import PartitionSpec as P


def broadcast(block, axis, owner):
    block = jnp.where(lax.axis_index(axis) == owner, block, jnp.zeros_like(block))
    return lax.psum(block, axis)


def build_mixing(peramb):
    real_part = peramb[0]
    imag_part = peramb[1]
    width = real_part.shape[0]
    upper = jnp.concatenate([real_part, -imag_part], axis=1)
    lower = jnp.concatenate([imag_part, real_part], axis=1)
    full = jnp.concatenate([upper, lower], axis=0)
    return full.reshape(2, width, 2, width)


def per_device(elemental, perambulators, source_owner):
    owner = source_owner[0]
    mine = perambulators[0]
    col_count = lax.axis_size("col")
    in_row = broadcast(mine, "col", owner % col_count)
    chosen = broadcast(in_row, "row", owner // col_count)
    mixing = build_mixing(chosen)
    first = jnp.einsum("scrk,rijk->sijc", mixing, elemental, preferred_element_type=jnp.float32)
    first = first.astype(jnp.bfloat16)
    result = jnp.einsum(
        "sbrj,rijc->sbic",
        mixing,
        lax.all_to_all(first, "col", split_axis=3, concat_axis=2, tiled=True),
        preferred_element_type=jnp.float32,
    )
    second = result.astype(jnp.bfloat16)
    return jnp.einsum(
        "sari,rbic->sabc",
        mixing,
        lax.all_to_all(second, "row", split_axis=1, concat_axis=2, tiled=True),
        preferred_element_type=jnp.float32,
    )


def solution(mesh):
    in_specs = (P(None, "row", "col", None), P(("row", "col"), None, None, None), P())
    out_specs = P(None, None, "row", "col")
    return jax.shard_map(
        per_device, mesh=mesh, in_specs=in_specs, out_specs=out_specs, check_vma=False
    )
```

profile of v0, /device:TPU:0, one launch (start us, length us, event | category | flops | bytes accessed | tf_op | source)
XLA Modules:
  0.0 885.9 jit_solution(7611328322135529125)
XLA Ops:
  6.5 0.0 all-reduce.3.cloned.1.call-start
  7.2 1.1 select_bitcast_fusion
  8.3 0.0 all-reduce.3.cloned.1.call-update
  8.3 0.0 all-reduce.5.cloned.1.call-start
  8.4 40.2 %all-reduce.3.cloned.1.call-done = bf16[2,512,512]{2,1,0:T(8,128)(2,1)} async-done(((bf16[2,512,512]{2,1,0:T(8,128)(2,1)}), bf16[2,512,512]{2,1,0:T(8,128)(2,1)}) %all-reduce.3.cloned.1.call-update) | async-done | bytes 1048592 | tf_op jit(solution)/shard_map/psum | solution.py:9
  48.6 1.0 broadcast_select_fusion
  49.6 0.0 all-reduce.5.cloned.1.call-update
  49.6 81.3 %all-reduce.5.cloned.1.call-done = bf16[2,512,512]{2,1,0:T(8,128)(2,1)} async-done(((bf16[2,512,512]{2,1,0:T(8,128)(2,1)}), bf16[2,512,512]{2,1,0:T(8,128)(2,1)}) %all-reduce.5.cloned.1.call-update) | async-done | bytes 1048592 | tf_op jit(solution)/shard_map/psum | solution.py:9
  130.9 1.1 fusion.8
  132.0 1.3 slice_bitcast_fusion
  133.3 0.3 maximum_maximum_fusion
  133.6 2.8 reshape.6
  136.3 21.3 %fusion.2 = bf16[2,64,128,512]{2,3,1,0:T(8,128)(2,1)S(1)} fusion(bf16[2,64,128,512]{3,2,1,0:T(8,128)(2,1)} %param.3, bf16[2,512,2,512,1]{3,2,1,0,4:T(2,128)(2,1)} %bitcast.52), kind=kOutput, calls=%fused_computation.5 | convolution fusion | flops 17188257792 | bytes 35651584 | tf_op jit(solution)/shard_map/scrk,rijk->sijc/dot_general | solution.py:29
  157.7 36.1 %copy.17 = bf16[2,64,128,512]{2,1,0,3:T(8,128)(2,1)S(1)} copy(bf16[2,64,128,512]{2,3,1,0:T(8,128)(2,1)S(1)} %fusion.2) | data formatting | bytes 33554432 | tf_op jit(solution)/shard_map/convert_element_type | solution.py:30
  193.8 187.4 %all_to_all.36 = bf16[2,64,128,512]{2,1,0,3:T(8,128)(2,1)} all-to-all(bf16[2,64,128,512]{2,1,0,3:T(8,128)(2,1)S(1)} %copy.17), channel_id=1, replica_groups=mesh['row'=8,'col'=4] {'col'}, dimensions={3} | all-to-all | bytes 33554432 | tf_op jit(solution)/shard_map/all_to_all | solution.py:34
  381.1 0.0 copy-start
  381.1 24.8 %copy.18 = bf16[2,64,128,4,128]{4,2,3,0,1:T(8,128)(2,1)} copy(bf16[2,64,128,4,128]{2,1,0,4,3:T(8,128)(2,1)} %bitcast.48) | data formatting | bytes 33554432 | tf_op jit(solution)/shard_map/all_to_all | solution.py:34
  406.0 0.0 copy-done
  406.0 25.9 %bitcast_convert_fusion = bf16[2,512,64,128]{3,1,2,0:T(8,128)(2,1)} fusion(bf16[2,64,512,128,1]{3,2,0,1,4:T(8,128)(2,1)} %bitcast.51, bf16[2,512,2,512,1]{3,2,1,0,4:T(2,128)(2,1)S(1)} %bitcast.53), kind=kOutput, calls=%fused_computation | convolution fusion | flops 17188257792 | bytes 35651584 | tf_op jit(solution)/shard_map/sbrj,rijc->sbic/dot_general | solution.py:31
  431.8 14.8 %copy.20 = bf16[2,512,64,128]{3,2,0,1:T(8,128)(2,1)S(1)} copy(bf16[2,512,64,128]{3,1,2,0:T(8,128)(2,1)} %bitcast_convert_fusion) | data formatting | bytes 33554432 | tf_op jit(solution)/shard_map/convert_element_type | solution.py:37
  446.6 367.1 %all_to_all.37 = bf16[2,512,64,128]{3,2,0,1:T(8,128)(2,1)S(1)} all-to-all(bf16[2,512,64,128]{3,2,0,1:T(8,128)(2,1)S(1)} %copy.20), channel_id=1, replica_groups=mesh['row'=8,'col'=4] {'row'}, dimensions={1} | all-to-all | bytes 33554432 | tf_op jit(solution)/shard_map/all_to_all | solution.py:41
  813.7 6.7 copy.21
  820.4 26.8 %convolution_bitcast_fusion = f32[2,512,64,128]{3,1,2,0:T(8,128)} fusion(bf16[2,64,512,128,1]{3,2,0,1,4:T(8,128)(2,1)} %bitcast.50, bf16[2,512,2,512,1]{3,2,1,0,4:T(2,128)(2,1)S(1)} %bitcast.54), kind=kOutput, calls=%fused_computation.2 | convolution fusion | flops 17179869184 | bytes 52428800 | tf_op jit(solution)/shard_map/sari,rbic->sabc/dot_general | solution.py:38
  847.2 31.9 %copy.23 = f32[2,512,64,128]{3,2,1,0:T(8,128)} copy(f32[2,512,64,128]{3,1,2,0:T(8,128)} %convolution_bitcast_fusion) | data formatting | bytes 67108864 | tf_op jit(solution)/shard_map/sari,rbic->sabc/dot_general | solution.py:38
Async XLA Ops:
  6.5 42.0 %all-reduce.3.cloned.1.call-start = ((), (), s32[]{:S(2)}) async-start(), calls=%async_computation.2 | async-start | bytes 2097152 | tf_op jit(solution)/shard_map/psum | solution.py:9
  8.3 122.6 %all-reduce.5.cloned.1.call-start = ((), (), s32[]{:S(2)}) async-start(), calls=%async_computation.3 | async-start | bytes 2097152 | tf_op jit(solution)/shard_map/psum | solution.py:9
  381.1 24.8 %copy-start = (bf16[2,512,2,512]{3,2,1,0:T(2,128)(2,1)S(1)}, bf16[2,512,2,512]{3,2,1,0:T(2,128)(2,1)}, u32[]{:S(2)}) copy-start(bf16[2,512,2,512]{3,2,1,0:T(2,128)(2,1)} %reshape.6) | copy-start | bytes 6291460
Sparse Core Ops, SparseCore 0:
  9.7 38.8 all-reduce.2
  52.5 78.3 all-reduce.4
where the time goes:
time: 887 us; the launch traced here: 886 us
  blocking collectives  554 us (62%)
  waiting for transfers between devices  122 us (14%)
  local copies, waits for them, and re-layouts  118 us (13%)
  matrix products  73.9 us (8%)
  between operations  14.1 us (2%)
    all_to_all x1, blocking collectives, per_device(): lax.all_to_all(second, 'row', split_axis=1, concat_axis=2, tiled=True)  367 us
    all_to_all x1, blocking collectives, per_device(): lax.all_to_all(first, 'col', split_axis=3, concat_axis=2, tiled=True)  187 us
    psum x2, waiting for transfers between devices, broadcast(): return lax.psum(block, axis)  121 us
    convert_element_type x1, local copies, waits for them, and re-layouts, per_device(): first = first.astype(jnp.bfloat16)  36.1 us
    dot_general x1, local copies, waits for them, and re-layouts, per_device(): jnp.einsum('sari,rbic->sabc', mixing, lax.all_to_all(second, 'row', split...  31.9 us
    dot_general x1, matrix products, per_device(): jnp.einsum('sari,rbic->sabc', mixing, lax.all_to_all(second, 'row', split...  26.8 us
    dot_general x1, matrix products, per_device(): jnp.einsum('sbrj,rijc->sbic', mixing, lax.all_to_all(first, 'col', split_...  25.9 us
    all_to_all x1, local copies, waits for them, and re-layouts, per_device(): lax.all_to_all(first, 'col', split_axis=3, concat_axis=2, tiled=True)  24.8 us
  transfers between devices with their start and end apart: 2, of which 2 were waited for; matrix products, arithmetic and copies ran while one was open for 0% of the time, Pallas kernels for 0%

commit v1 on v0

v1 whole, which is shorter than its diff:
```python
import functools

import jax
import jax.numpy as jnp
from jax import lax
from jax.experimental import pallas as pl
from jax.experimental.pallas import tpu as pltpu
from jax.sharding import PartitionSpec as P

VMEM_BYTES = 56 * 1024 * 1024


def is_power_of_two(n):
    return n & (n - 1) == 0


def flip(n, bit):
    return [(i, i ^ bit) for i in range(n)]


def take_from_owner(block, axis, bit, owner):
    received = lax.ppermute(block, axis, flip(lax.axis_size(axis), bit))
    return jnp.where((lax.axis_index(axis) & bit) == (owner & bit), block, received)


def broadcast_rows(block, owner_row, owner_col):
    row_count, col_count = lax.axis_size("row"), lax.axis_size("col")
    if not (is_power_of_two(row_count) and is_power_of_two(col_count)):
        mine = (lax.axis_index("row") == owner_row) & (lax.axis_index("col") == owner_col)
        return lax.psum(jnp.where(mine, block, jnp.zeros_like(block)), ("row", "col"))
    steps = [("row", 1 << n, owner_row) for n in range(row_count.bit_length() - 1)]
    steps += [("col", 1 << n, owner_col) for n in range(1, col_count.bit_length() - 1)]
    paired = col_count > 1
    whole = block
    if paired:
        whole = take_from_owner(block, "col", 1, owner_col)
        half = block.shape[0] // 2
        low = (lax.axis_index("col") & 1) == 0
        block = jnp.where(low, whole[:half], whole[half:])
    pieces = 3
    rows = block.shape[0]
    cuts = [rows * p // pieces // 16 * 16 for p in range(pieces)] + [rows]
    parts = [block[cuts[p] : cuts[p + 1]] for p in range(pieces)]
    for n in range(len(steps)):
        for p in range(pieces):
            axis, bit, owner = steps[(n + p) % len(steps)]
            parts[p] = take_from_owner(parts[p], axis, bit, owner)
    block = jnp.concatenate(parts)
    if paired:
        other = lax.ppermute(block, "col", flip(col_count, 1))
        block = jnp.concatenate([jnp.where(low, block, other), jnp.where(low, other, block)])
    return block


def first_kernel(place, mixing, elem, *outs):
    width = elem.shape[-1]
    count, local_j = elem.shape[1], elem.shape[2]
    cols = outs[0].shape[-1]
    left = jnp.concatenate(
        [elem[0].reshape(count * local_j, width), elem[1].reshape(count * local_j, width)], axis=1
    )
    for t, out in enumerate(outs):
        start = pl.multiple_of((place[1] ^ t) * cols, cols)
        right = jnp.concatenate(
            [mixing[pl.ds(start, cols), :], mixing[pl.ds(width + start, cols), :]], axis=0
        )
        res = lax.dot_general(
            left, right, (((1,), (1,)), ((), ())), preferred_element_type=jnp.float32
        ).astype(jnp.bfloat16)
        for s in range(2):
            out[s] = res[:, s * cols : (s + 1) * cols].reshape(count, local_j, cols)


def contract_first(mixing, elemental, place, offset, count, col_count):
    _, _, local_j, width = elemental.shape
    cols = width // col_count
    step = count if offset == 0 else min(offset, count)
    while count % step or offset % step or step > 4:
        step -= 1
    out_shape = jax.ShapeDtypeStruct((2, count, local_j, cols), jnp.bfloat16)
    return pl.pallas_call(
        first_kernel,
        name="first",
        grid=(count // step,),
        in_specs=[
            pl.BlockSpec(memory_space=pltpu.SMEM),
            pl.BlockSpec(mixing.shape, lambda n: (0, 0)),
            pl.BlockSpec((2, step, local_j, width), lambda n: (0, offset // step + n, 0, 0)),
        ],
        out_specs=[pl.BlockSpec((2, step, local_j, cols), lambda n: (0, n, 0, 0))] * col_count,
        out_shape=[out_shape] * col_count,
        compiler_params=pltpu.CompilerParams(vmem_limit_bytes=VMEM_BYTES),
        cost_estimate=pl.CostEstimate(
            flops=8 * count * local_j * width * width,
            bytes_accessed=8 * count * local_j * width + 8 * width * width,
            transcendentals=0,
        ),
    )(place, mixing, elemental)


def second_kernel(col_count, row_count, splits, place, mixing, *refs):
    blocks, outs, (ordered, right) = refs[:col_count], refs[col_count:-2], refs[-2:]
    width = mixing.shape[0] // 2
    _, count, local_j, cols = blocks[0].shape
    local_b = width // row_count

    @pl.when(pl.program_id(0) == 0)
    def _():
        for t in range(row_count):
            start = pl.multiple_of((place[0] ^ t) * local_b, local_b)
            for s in range(2):
                ordered[pl.ds((2 * t + s) * local_b, local_b), :] = mixing[
                    pl.ds(s * width + start, local_b), :
                ]

    for t, block in enumerate(blocks):
        start = pl.multiple_of((place[1] ^ t) * local_j, local_j)
        for r in range(2):
            for i in range(count):
                right[pl.ds(r * width + start, local_j), i * cols : (i + 1) * cols] = block[r, i]
    res = jnp.dot(ordered[...], right[...], preferred_element_type=jnp.float32)
    res = res.astype(jnp.bfloat16)
    part = local_b // splits
    for u in range(splits):
        for t in range(row_count):
            for s in range(2):
                row = (2 * t + s) * local_b + u * part
                for i in range(count):
                    outs[u * row_count + t][s, i] = res[
                        row : row + part, i * cols : (i + 1) * cols
                    ]


def contract_second(mixing, blocks, place, row_count, splits):
    col_count = len(blocks)
    _, count, local_j, cols = blocks[0].shape
    width = mixing.shape[0] // 2
    part = width // row_count // splits
    step = min(count, 4)
    while count % step:
        step -= 1
    out_shape = jax.ShapeDtypeStruct((2, count, part, cols), jnp.bfloat16)
    outs = pl.pallas_call(
        functools.partial(second_kernel, col_count, row_count, splits),
        name="second",
        grid=(count // step,),
        in_specs=[
            pl.BlockSpec(memory_space=pltpu.SMEM),
            pl.BlockSpec(mixing.shape, lambda n: (0, 0)),
        ]
        + [pl.BlockSpec((2, step, local_j, cols), lambda n: (0, n, 0, 0))] * col_count,
        out_specs=[pl.BlockSpec((2, step, part, cols), lambda n: (0, n, 0, 0))]
        * (row_count * splits),
        out_shape=[out_shape] * (row_count * splits),
        scratch_shapes=[
            pltpu.VMEM(mixing.shape, jnp.bfloat16),
            pltpu.VMEM((2 * width, step * cols), jnp.bfloat16),
        ],
        compiler_params=pltpu.CompilerParams(vmem_limit_bytes=VMEM_BYTES),
        cost_estimate=pl.CostEstimate(
            flops=8 * count * cols * width * width,
            bytes_accessed=8 * count * cols * width + 8 * width * width,
            transcendentals=0,
        ),
    )(place, mixing, *blocks)
    return [outs[u * row_count : (u + 1) * row_count] for u in range(splits)]


def third_kernel(row_count, offsets, rows, aliased, place, mixing, *refs):
    total = row_count * len(offsets)
    blocks, (out, gathered) = refs[:total], refs[total + aliased :]
    width = mixing.shape[0] // 2
    local_i = width // row_count
    depth, part, cols = gathered.shape

    @pl.when(pl.program_id(0) == 0)
    def _():
        for n, block in enumerate(blocks):
            chunk, t = divmod(n, row_count)
            source = place[0] ^ t
            for r in range(2):
                start = r * width + source * local_i + offsets[chunk]
                gathered[pl.ds(start, block.shape[1])] = block[r].astype(jnp.float32)

    flat = gathered.reshape(depth * part, cols)
    result = out.reshape(depth * rows, cols)
    base = pl.program_id(0) * rows
    for b in range(0, rows, 2):
        right = jnp.concatenate(
            [
                flat[pl.ds(base + b + n, depth, stride=part), :].astype(jnp.bfloat16)
                for n in range(2)
            ],
            axis=1,
        )
        res = jnp.dot(mixing[...], right, preferred_element_type=jnp.float32)
        for n in range(2):
            result[pl.ds(b + n, depth, stride=rows), :] = res[:, n * cols : (n + 1) * cols]


def contract_third(mixing, chunks, place, offsets, index, splits, previous):
    row_count = len(chunks[0])
    depth = mixing.shape[0]
    cols = chunks[0][0].shape[-1]
    part = chunks[-1][0].shape[2]
    rows = 8
    in_specs = [
        pl.BlockSpec(memory_space=pltpu.SMEM),
        pl.BlockSpec(mixing.shape, lambda n: (0, 0)),
    ]
    operands = [place, mixing]
    for q, chunk in enumerate(chunks):
        where = index if chunk[0].shape[2] != part else 0
        for block in chunk:
            shape = (2, block.shape[1], part, cols)
            in_specs.append(pl.BlockSpec(shape, lambda n, where=where: (0, 0, where, 0)))
            operands.append(block)
    aliases = {}
    if previous is not None:
        aliases = {len(operands): 0}
        in_specs.append(pl.BlockSpec(memory_space=pl.ANY))
        operands.append(previous)
    return pl.pallas_call(
        functools.partial(third_kernel, row_count, offsets, rows, len(aliases)),
        name="third",
        grid=(part // rows,),
        in_specs=in_specs,
        out_specs=pl.BlockSpec((depth, rows, cols), lambda n: (0, index * (part // rows) + n, 0)),
        out_shape=jax.ShapeDtypeStruct((depth, part * splits, cols), jnp.float32),
        scratch_shapes=[pltpu.VMEM((depth, part, cols), jnp.float32)],
        input_output_aliases=aliases,
        compiler_params=pltpu.CompilerParams(vmem_limit_bytes=VMEM_BYTES),
        cost_estimate=pl.CostEstimate(
            flops=2 * depth * depth * part * cols,
            bytes_accessed=6 * depth * part * cols + 2 * depth * depth,
            transcendentals=0,
        ),
    )(*operands)


def build_mixing(peramb):
    real_part, imag_part = peramb
    upper = jnp.concatenate([real_part, -imag_part], axis=1)
    lower = jnp.concatenate([imag_part, real_part], axis=1)
    return jnp.concatenate([upper, lower], axis=0)


class Lane:
    def __init__(self, axis, depth):
        self.axis = axis
        self.depth = depth
        self.results = []

    def send(self, block, bit):
        if len(self.results) >= self.depth:
            block, _ = lax.optimization_barrier((block, self.results[-self.depth]))
        result = lax.ppermute(block, self.axis, flip(lax.axis_size(self.axis), bit))
        self.results.append(result)
        return result


def after(value, *others):
    if not others:
        return value
    return lax.optimization_barrier((value, others))[0]


def per_device(elemental, perambulators, source_owner):
    owner = source_owner[0]
    row_count, col_count = lax.axis_size("row"), lax.axis_size("col")
    place = jnp.stack([lax.axis_index("row"), lax.axis_index("col")]).astype(jnp.int32)
    _, local_i, local_j, width = elemental.shape
    local_b, cols = width // row_count, width // col_count
    chosen = broadcast_rows(
        perambulators[0].reshape(2 * width, width), owner // col_count, owner % col_count
    )
    mixing = build_mixing(chosen.reshape(2, width, width))

    if cols % 128 or local_b % 16 or local_i % 16 or not is_power_of_two(row_count * col_count):
        mixing = mixing.reshape(2, width, 2, width)
        first = jnp.einsum("scrk,rijk->sijc", mixing, elemental, preferred_element_type=jnp.float32)
        first = lax.all_to_all(first.astype(jnp.bfloat16), "col", 3, 2, tiled=True)
        second = jnp.einsum("sbrj,rijc->sbic", mixing, first, preferred_element_type=jnp.float32)
        second = lax.all_to_all(second.astype(jnp.bfloat16), "row", 1, 2, tiled=True)
        return jnp.einsum("sari,rbic->sabc", mixing, second, preferred_element_type=jnp.float32)

    counts = [local_i // 16, local_i // 8, local_i * 5 // 16]
    counts.append(local_i - sum(counts))
    offsets = [sum(counts[:q]) for q in range(len(counts))]
    splits = local_b // 16
    half = row_count // 2
    order = [half] + [t for n in range(1, half) for t in (n, half + n)]
    col_lane, row_lane = Lane("col", 2), Lane("row", 3)
    last = len(counts) - 1
    firsts, chunks, tails = {}, [], []

    def start(q, token, wait):
        blocks = contract_first(mixing, elemental, after(place, token), offsets[q], counts[q], col_count)
        blocks = after(blocks, *wait)
        firsts[q] = [blocks[0]] + [col_lane.send(blocks[t], t) for t in range(1, col_count)]

    start(0, mixing, [])
    start(1, mixing, [])
    for q in range(len(counts)):
        parts = contract_second(
            mixing, firsts[q], place, row_count, splits if q == last else 1
        )
        for part in parts:
            arrived = {0: part[0]}
            for t in order:
                arrived[t] = row_lane.send(part[t], t)
            (tails if q == last else chunks).append([arrived[t] for t in range(row_count)])
        if q + 2 <= last:
            start(q + 2, parts[0][0], [arrived[t] for t in order])
    result = None
    for u, tail in enumerate(tails):
        result = contract_third(mixing, chunks + [tail], place, offsets, u, splits, result)
    return result.reshape(2, width, local_b, cols)


def solution(mesh):
    in_specs = (P(None, "row", "col", None), P(("row", "col"), None, None, None), P())
    out_specs = P(None, None, "row", "col")
    return jax.shard_map(
        per_device, mesh=mesh, in_specs=in_specs, out_specs=out_specs, check_vma=False
    )
```

time: 887 us -> 529 us (0.60)
  blocking collectives: 554 us -> 0 us
  starting transfers between devices: 0.04 us -> 153 us
  waiting for transfers between devices: 122 us -> 247 us
  Pallas kernels: 0 us -> 118 us
  local copies, waits for them, and re-layouts: 118 us -> 1.93 us
  matrix products: 73.9 us -> 0 us
  between operations: 14.1 us -> 1.86 us
    all_to_all x2 -> x0, blocking collectives: 554 us -> none  [the longest x1 367 us: per_device(): lax.all_to_all(second, 'row', split_axis=1, concat_axis=2, tiled=True)]
    ppermute x0 -> x75, waiting for transfers between devices: none -> 247 us  [the longest x61 219 us: send(): result = lax.ppermute(block, self.axis, flip(lax.axis_size(self.axis), bit))]
    ppermute x0 -> x75, starting transfers between devices: none -> 153 us  [the longest x61 133 us: send(): result = lax.ppermute(block, self.axis, flip(lax.axis_size(self.axis), bit))]
    psum x2 -> x0, waiting for transfers between devices: 121 us -> none  [broadcast(): return lax.psum(block, axis)]
    pallas_call x0 -> x12, Pallas kernels: none -> 118 us  [the longest x4 46.2 us: contract_third(): pl.pallas_call(functools.partial(third_kernel, row_count, offsets, rows,...]
    dot_general x3 -> x0, matrix products: 73.9 us -> none  [the longest x1 26.8 us: per_device(): jnp.einsum('sari,rbic->sabc', mixing, lax.all_to_all(second, 'row', split...]
    convert_element_type x2 -> x0, local copies, waits for them, and re-layouts: 50.9 us -> none  [the longest x1 36.1 us: per_device(): first = first.astype(jnp.bfloat16)]
    dot_general x1 -> x0, local copies, waits for them, and re-layouts: 31.9 us -> none  [per_device(): jnp.einsum('sari,rbic->sabc', mixing, lax.all_to_all(second, 'row', split...]
  transfers between devices with their start and end apart: 2 -> 75, of which waited for: 2 -> 34; matrix products, arithmetic and copies ran while one was open for 0% -> 0% of each run, Pallas kernels for 0% -> 20%
where the time goes in v1:
time: 529 us; the launch traced here: 525 us
  waiting for transfers between devices  247 us (47%)
  starting transfers between devices  153 us (29%)
  Pallas kernels  118 us (22%)
    ppermute x61, waiting for transfers between devices, send(): result = lax.ppermute(block, self.axis, flip(lax.axis_size(self.axis), bit))  219 us
    ppermute x61, starting transfers between devices, send(): result = lax.ppermute(block, self.axis, flip(lax.axis_size(self.axis), bit))  133 us
    pallas_call x4, Pallas kernels, contract_third(): pl.pallas_call(functools.partial(third_kernel, row_count, offsets, rows,...  46.2 us
    pallas_call x4, Pallas kernels, contract_second(): pl.pallas_call(functools.partial(second_kernel, col_count, row_count, spl...  37.7 us
    pallas_call x4, Pallas kernels, contract_first(): pl.pallas_call(first_kernel, name='first', grid=(count // step,), in_spec...  34.3 us
    ppermute x13, waiting for transfers between devices, take_from_owner(): received = lax.ppermute(block, axis, flip(lax.axis_size(axis), bit))  25.9 us
    ppermute x13, starting transfers between devices, take_from_owner(): received = lax.ppermute(block, axis, flip(lax.axis_size(axis), bit))  19.3 us
  transfers between devices with their start and end apart: 75, of which 34 were waited for; matrix products, arithmetic and copies ran while one was open for 0% of the time, Pallas kernels for 20%

profile of v1, /device:TPU:0, one launch (start us, length us, event | category | flops | bytes accessed | tf_op | source)
XLA Modules:
  0.0 525.5 jit_solution(3233593954822776065)
XLA Ops:
  24.8 9.0 %collective-permute-done.6 = bf16[176,512]{1,0:T(8,128)(2,1)S(1)} collective-permute-done((bf16[176,512]{1,0:T(8,128)(2,1)S(1)}, bf16[176,512]{1,0:T(8,128)(2,1)S(1)}, u32[]{:S(2)}, u32[]{:S(2)}) %collective-permute-start.6) | collective-permute-done | bytes 180256 | tf_op jit(solution)/shard_map/ppermute | solution.py:22
  56.2 5.8 %first.5 = (bf16[2,8,128,128]{3,2,1,0:T(8,128)(2,1)}, bf16[2,8,128,128]{3,2,1,0:T(8,128)(2,1)}, bf16[2,8,128,128]{3,2,1,0:T(8,128)(2,1)}, bf16[2,8,128,128]{3,2,1,0:T(8,128)(2,1)}) custom-call(s32[2]{0:T(128)} %pad_add_fusion.place, bf16[1024,1024]{1,0:T(8,128)(2,1)} %maximum_maximum_fusion.mixing, bf16[2,64,128,512]{3,2,1,0:T(8,128)(2,1)} %elem.7), custom_call_target="tpu_custom_call" | custom-call | flops 2147483648 | bytes 6291456 | tf_op jit(solution)/shard_map/first/pallas_call | solution.py:81
  65.0 7.3 %collective-permute-done.16.refs_3_ = bf16[2,4,128,128]{3,2,1,0:T(8,128)(2,1)S(1)} collective-permute-done((bf16[2,4,128,128]{3,2,1,0:T(8,128)(2,1)S(1)}, bf16[2,4,128,128]{3,2,1,0:T(8,128)(2,1)S(1)}, u32[]{:S(2)}, u32[]{:S(2)}) %collective-permute-start.16) | collective-permute-done | bytes 262176 | tf_op jit(solution)/shard_map/ppermute | solution.py:257
  82.5 7.6 %collective-permute-done.18.refs_4_ = bf16[2,4,64,128]{3,2,1,0:T(8,128)(2,1)S(1)} collective-permute-done((bf16[2,4,64,128]{3,2,1,0:T(8,128)(2,1)}, bf16[2,4,64,128]{3,2,1,0:T(8,128)(2,1)S(1)}, u32[]{:S(2)}, u32[]{:S(2)}) %collective-permute-start.18) | collective-permute-done | bytes 131104 | tf_op jit(solution)/shard_map/ppermute | solution.py:257
  98.7 6.1 %second.5 = (bf16[2,8,64,128]{3,2,1,0:T(8,128)(2,1)}, bf16[2,8,64,128]{3,2,1,0:T(8,128)(2,1)}, bf16[2,8,64,128]{3,2,1,0:T(8,128)(2,1)}, bf16[2,8,64,128]{3,2,1,0...) custom-call(s32[2]{0:T(128)} %pad_add_fusion.place, ...), custom_call_target="tpu_custom_call" | custom-call | flops 2147483648 | bytes 6291456 | tf_op jit(solution)/shard_map/second/pallas_call | solution.py:143
  105.4 10.1 %first.6 = (bf16[2,20,128,128]{3,2,1,0:T(8,128)(2,1)}, bf16[2,20,128,128]{3,2,1,0:T(8,128)(2,1)}, bf16[2,20,128,128]{3,2,1,0:T(8,128)(2,1)}, bf16[2,20,128,128]{3,2,1,0:T(8,128)(2,1)}) custom-call(s32[2]{0:T(128)} %pad_add_fusion.place, bf16[1024,1024]{1,0:T(8,128)(2,1)} %maximum_maximum_fusion.mixing, bf16[2,64,128,512]{3,2,1,0:T(8,128)(2,1)} %elem.7), custom_call_target="tpu_custom_call" | custom-call | flops 5368709120 | bytes 12582912 | tf_op jit(solution)/shard_map/first/pallas_call | solution.py:81
  121.4 10.1 %collective-permute-done.30.refs_13_ = bf16[2,8,64,128]{3,2,1,0:T(8,128)(2,1)S(1)} collective-permute-done((bf16[2,8,64,128]{3,2,1,0:T(8,128)(2,1)S(1)}, bf16[2,8,64,128]{3,2,1,0:T(8,128)(2,1)S(1)}, u32[]{:S(2)}, u32[]{:S(2)}) %collective-permute-start.30) | collective-permute-done | bytes 262176 | tf_op jit(solution)/shard_map/ppermute | solution.py:257
  136.5 14.5 %first.7 = (bf16[2,32,128,128]{3,2,1,0:T(8,128)(2,1)}, bf16[2,32,128,128]{3,2,1,0:T(8,128)(2,1)}, bf16[2,32,128,128]{3,2,1,0:T(8,128)(2,1)}, bf16[2,32,128,128]{3,2,1,0:T(8,128)(2,1)}) custom-call(s32[2]{0:T(128)} %pad_add_fusion.place, bf16[1024,1024]{1,0:T(8,128)(2,1)} %maximum_maximum_fusion.mixing, bf16[2,64,128,512]{3,2,1,0:T(8,128)(2,1)} %elem.7), custom_call_target="tpu_custom_call" | custom-call | flops 8589934592 | bytes 18874368 | tf_op jit(solution)/shard_map/first/pallas_call | solution.py:81
  152.3 29.5 %collective-permute-done.36.refs_3_ = bf16[2,20,128,128]{3,2,1,0:T(8,128)(2,1)S(1)} collective-permute-done((bf16[2,20,128,128]{3,2,1,0:T(8,128)(2,1)S(1)}, bf16[2,20,128,128]{3,2,1,0:T(8,128)(2,1)S(1)}, u32[]{:S(2)}, u32[]{:S(2)}) %collective-permute-start.36) | collective-permute-done | bytes 1310752 | tf_op jit(solution)/shard_map/ppermute | solution.py:257
  183.6 10.7 %second.6 = (bf16[2,20,64,128]{3,2,1,0:T(8,128)(2,1)}, bf16[2,20,64,128]{3,2,1,0:T(8,128)(2,1)}, bf16[2,20,64,128]{3,2,1,0:T(8,128)(2,1)}, bf16[2,20,64,128]{3,2...) custom-call(s32[2]{0:T(128)} %pad_add_fusion.place, ...), custom_call_target="tpu_custom_call" | custom-call | flops 5368709120 | bytes 12582912 | tf_op jit(solution)/shard_map/second/pallas_call | solution.py:143
  194.4 7.2 %collective-permute-start.38 = (bf16[2,20,64,128]{3,2,1,0:T(8,128)(2,1)}, bf16[2,20,64,128]{3,2,1,0:T(8,128)(2,1)S(1)}, u32[]{:S(2)}, u32[]{:S(2)}) collective-permute-start(bf16[2,20,64,128]{3,2,1,0:T(8,128)(2,1)} %get-tuple-element.201), channel_id=1, source_target_pairs={{0,16},{4,20},{8,24},{12,28},{16,0},{20,4},{24,8},{28,12},{1,17},{... | collective-permute-start | bytes 1966088 | tf_op jit(solution)/shard_map/ppermute | solution.py:257
  203.1 42.3 %collective-permute-done.38.refs_20_ = bf16[2,20,64,128]{3,2,1,0:T(8,128)(2,1)S(1)} collective-permute-done((bf16[2,20,64,128]{3,2,1,0:T(8,128)(2,1)}, bf16[2,20,64,128]{3,2,1,0:T(8,128)(2,1)S(1)}, u32[]{:S(2)}, u32[]{:S(2)}) %collective-permute-start.38) | collective-permute-done | bytes 655392 | tf_op jit(solution)/shard_map/ppermute | solution.py:257
  245.4 14.8 %collective-permute-done.40.refs_21_ = bf16[2,20,64,128]{3,2,1,0:T(8,128)(2,1)S(1)} collective-permute-done((bf16[2,20,64,128]{3,2,1,0:T(8,128)(2,1)}, bf16[2,20,64,128]{3,2,1,0:T(8,128)(2,1)S(1)}, u32[]{:S(2)}, u32[]{:S(2)}) %collective-permute-start.40) | collective-permute-done | bytes 655392 | tf_op jit(solution)/shard_map/ppermute | solution.py:257
  262.5 10.7 %collective-permute-done.39.refs_18_ = bf16[2,20,64,128]{3,2,1,0:T(8,128)(2,1)S(1)} collective-permute-done((bf16[2,20,64,128]{3,2,1,0:T(8,128)(2,1)}, bf16[2,20,64,128]{3,2,1,0:T(8,128)(2,1)S(1)}, u32[]{:S(2)}, u32[]{:S(2)}) %collective-permute-start.39) | collective-permute-done | bytes 655392 | tf_op jit(solution)/shard_map/ppermute | solution.py:257
  276.5 16.8 %second.7 = (bf16[2,32,16,128]{3,2,1,0:T(8,128)(2,1)}, bf16[2,32,16,128]{3,2,1,0:T(8,128)(2,1)}, bf16[2,32,16,128]{3,2,1,0:T(8,128)(2,1)}, bf16[2,32,16,128]{3,2...) custom-call(s32[2]{0:T(128)} %pad_add_fusion.place, ...), custom_call_target="tpu_custom_call" | custom-call | flops 8589934592 | bytes 18874368 | tf_op jit(solution)/shard_map/second/pallas_call | solution.py:143
  293.4 18.3 %collective-permute-start.55 = (bf16[2,32,16,128]{3,2,1,0:T(8,128)(2,1)}, bf16[2,32,16,128]{3,2,1,0:T(8,128)(2,1)S(1)}, u32[]{:S(2)}, u32[]{:S(2)}) collective-permute-start(bf16[2,32,16,128]{3,2,1,0:T(8,128)(2,1)} %get-tuple-element.249), channel_id=1, source_target_pairs={{0,16},{4,20},{8,24},{12,28},{16,0},{20,4},{24,8},{28,12},{1,17},{... | collective-permute-start | bytes 786440 | tf_op jit(solution)/shard_map/ppermute | solution.py:257
  311.6 17.8 %collective-permute-start.64 = (bf16[2,32,16,128]{3,2,1,0:T(8,128)(2,1)}, bf16[2,32,16,128]{3,2,1,0:T(8,128)(2,1)S(1)}, u32[]{:S(2)}, u32[]{:S(2)}) collective-permute-start(bf16[2,32,16,128]{3,2,1,0:T(8,128)(2,1)} %get-tuple-element.267), channel_id=1, source_target_pairs={{0,20},{4,16},{8,28},{12,24},{16,4},{20,0},{24,12},{28,8},{1,21},{... | collective-permute-start | bytes 786440 | tf_op jit(solution)/shard_map/ppermute | solution.py:257
  331.0 7.6 %collective-permute-done.55.refs_28_ = bf16[2,32,16,128]{3,2,1,0:T(8,128)(2,1)S(1)} collective-permute-done((bf16[2,32,16,128]{3,2,1,0:T(8,128)(2,1)}, bf16[2,32,16,128]{3,2,1,0:T(8,128)(2,1)S(1)}, u32[]{:S(2)}, u32[]{:S(2)}) %collective-permute-start.55) | collective-permute-done | bytes 262176 | tf_op jit(solution)/shard_map/ppermute | solution.py:257
  351.5 14.2 %collective-permute-done.65.refs_27_ = bf16[2,32,16,128]{3,2,1,0:T(8,128)(2,1)S(1)} collective-permute-done((bf16[2,32,16,128]{3,2,1,0:T(8,128)(2,1)}, bf16[2,32,16,128]{3,2,1,0:T(8,128)(2,1)S(1)}, u32[]{:S(2)}, u32[]{:S(2)}) %collective-permute-start.65) | collective-permute-done | bytes 262176 | tf_op jit(solution)/shard_map/ppermute | solution.py:257
  373.7 8.9 %collective-permute-start.67 = (bf16[2,32,16,128]{3,2,1,0:T(8,128)(2,1)}, bf16[2,32,16,128]{3,2,1,0:T(8,128)(2,1)S(1)}, u32[]{:S(2)}, u32[]{:S(2)}) collective-permute-start(bf16[2,32,16,128]{3,2,1,0:T(8,128)(2,1)} %get-tuple-element.270), channel_id=1, source_target_pairs={{0,24},{4,28},{8,16},{12,20},{16,8},{20,12},{24,0},{28,4},{1,25},{... | collective-permute-start | bytes 786440 | tf_op jit(solution)/shard_map/ppermute | solution.py:257
  382.6 8.6 %collective-permute-done.49.refs_28_ = bf16[2,32,16,128]{3,2,1,0:T(8,128)(2,1)S(1)} collective-permute-done((bf16[2,32,16,128]{3,2,1,0:T(8,128)(2,1)}, bf16[2,32,16,128]{3,2,1,0:T(8,128)(2,1)S(1)}, u32[]{:S(2)}, u32[]{:S(2)}) %collective-permute-start.49) | collective-permute-done | bytes 262176 | tf_op jit(solution)/shard_map/ppermute | solution.py:257
  391.1 6.7 %collective-permute-done.58.refs_29_ = bf16[2,32,16,128]{3,2,1,0:T(8,128)(2,1)S(1)} collective-permute-done((bf16[2,32,16,128]{3,2,1,0:T(8,128)(2,1)}, bf16[2,32,16,128]{3,2,1,0:T(8,128)(2,1)S(1)}, u32[]{:S(2)}, u32[]{:S(2)}) %collective-permute-start.58) | collective-permute-done | bytes 262176 | tf_op jit(solution)/shard_map/ppermute | solution.py:257
  397.9 5.5 %collective-permute-start.68 = (bf16[2,32,16,128]{3,2,1,0:T(8,128)(2,1)}, bf16[2,32,16,128]{3,2,1,0:T(8,128)(2,1)S(1)}, u32[]{:S(2)}, u32[]{:S(2)}) collective-permute-start(bf16[2,32,16,128]{3,2,1,0:T(8,128)(2,1)} %get-tuple-element.271), channel_id=1, source_target_pairs={{0,16},{4,20},{8,24},{12,28},{16,0},{20,4},{24,8},{28,12},{1,17},{... | collective-permute-start | bytes 786440 | tf_op jit(solution)/shard_map/ppermute | solution.py:257
  411.3 10.8 %collective-permute-done.68.refs_28_ = bf16[2,32,16,128]{3,2,1,0:T(8,128)(2,1)S(1)} collective-permute-done((bf16[2,32,16,128]{3,2,1,0:T(8,128)(2,1)}, bf16[2,32,16,128]{3,2,1,0:T(8,128)(2,1)S(1)}, u32[]{:S(2)}, u32[]{:S(2)}) %collective-permute-start.68) | collective-permute-done | bytes 262176 | tf_op jit(solution)/shard_map/ppermute | solution.py:257
  422.0 6.8 %collective-permute-start.52 = (bf16[2,32,16,128]{3,2,1,0:T(8,128)(2,1)}, bf16[2,32,16,128]{3,2,1,0:T(8,128)(2,1)S(1)}, u32[]{:S(2)}, u32[]{:S(2)}) collective-permute-start(bf16[2,32,16,128]{3,2,1,0:T(8,128)(2,1)} %get-tuple-element.237), channel_id=1, source_target_pairs={{0,20},{4,16},{8,28},{12,24},{16,4},{20,0},{24,12},{28,8},{1,21},{... | collective-permute-start | bytes 786440 | tf_op jit(solution)/shard_map/ppermute | solution.py:257
  434.7 18.4 %collective-permute-done.52.refs_29_ = bf16[2,32,16,128]{3,2,1,0:T(8,128)(2,1)S(1)} collective-permute-done((bf16[2,32,16,128]{3,2,1,0:T(8,128)(2,1)}, bf16[2,32,16,128]{3,2,1,0:T(8,128)(2,1)S(1)}, u32[]{:S(2)}, u32[]{:S(2)}) %collective-permute-start.52) | collective-permute-done | bytes 262176 | tf_op jit(solution)/shard_map/ppermute | solution.py:257
  453.1 6.8 %collective-permute-start.62 = (bf16[2,32,16,128]{3,2,1,0:T(8,128)(2,1)}, bf16[2,32,16,128]{3,2,1,0:T(8,128)(2,1)S(1)}, u32[]{:S(2)}, u32[]{:S(2)}) collective-permute-start(bf16[2,32,16,128]{3,2,1,0:T(8,128)(2,1)} %get-tuple-element.256), channel_id=1, source_target_pairs={{0,16},{4,20},{8,24},{12,28},{16,0},{20,4},{24,8},{28,12},{1,17},{... | collective-permute-start | bytes 786440 | tf_op jit(solution)/shard_map/ppermute | solution.py:257
  460.0 11.5 %third.4.refs_32_ = f32[1024,64,128]{2,1,0:T(8,128)} custom-call(s32[2]{0:T(128)} %pad_add_fusion.place, bf16[1024,1024]{1,0:T(8,128)(2,1)} %maximum_maximum_fusion.mixing, bf16[2,4,64,128]{3,2,1,0:T(8,128)(2,1)} %get-tuple-element.150.refs_0_, bf16[2,4,64,128]{3,2,1,0:T(8,128)(2,1)} %copy-done.15, bf16[2,4,64,128]{3,2,1,0:T(8,128)(2,1)} %copy-done.17, ...), custom_call_target="tpu_custom_call" | custom-call | flops 4294967296 | bytes 14680064 | tf_op jit(solution)/shard_map/third/pallas_call | solution.py:223
  473.4 8.5 %collective-permute-done.62.refs_28_ = bf16[2,32,16,128]{3,2,1,0:T(8,128)(2,1)S(1)} collective-permute-done((bf16[2,32,16,128]{3,2,1,0:T(8,128)(2,1)}, bf16[2,32,16,128]{3,2,1,0:T(8,128)(2,1)S(1)}, u32[]{:S(2)}, u32[]{:S(2)}) %collective-permute-start.62) | collective-permute-done | bytes 262176 | tf_op jit(solution)/shard_map/ppermute | solution.py:257
  482.0 11.6 %third.5.refs_32_ = f32[1024,64,128]{2,1,0:T(8,128)} custom-call(s32[2]{0:T(128)} %pad_add_fusion.place, bf16[1024,1024]{1,0:T(8,128)(2,1)} %maximum_maximum_fusion.mixing, bf16[2,4,64,128]{3,2,1,0:T(8,128)(2,1)} %get-tuple-element.150.refs_0_, bf16[2,4,64,128]{3,2,1,0:T(8,128)(2,1)} %copy-done.15, ...), custom_call_target="tpu_custom_call", output_to_operand_aliasing={{}: (34, {})} | custom-call | flops 4294967296 | bytes 14680064 | tf_op jit(solution)/shard_map/third/pallas_call | solution.py:223
  500.4 11.7 %third.6.refs_32_ = f32[1024,64,128]{2,1,0:T(8,128)} custom-call(s32[2]{0:T(128)} %pad_add_fusion.place, bf16[1024,1024]{1,0:T(8,128)(2,1)} %maximum_maximum_fusion.mixing, bf16[2,4,64,128]{3,2,1,0:T(8,128)(2,1)} %get-tuple-element.150.refs_0_, bf16[2,4,64,128]{3,2,1,0:T(8,128)(2,1)} %copy-done.15, ...), custom_call_target="tpu_custom_call", output_to_operand_aliasing={{}: (34, {})} | custom-call | flops 4294967296 | bytes 14680064 | tf_op jit(solution)/shard_map/third/pallas_call | solution.py:223
  513.9 11.4 %third.7 = f32[1024,64,128]{2,1,0:T(8,128)} custom-call(s32[2]{0:T(128)} %pad_add_fusion.place, bf16[1024,1024]{1,0:T(8,128)(2,1)} %maximum_maximum_fusion.mixing, bf16[2,4,64,128]{3,2,1,0:T(8,128)(2,1)} %get-tuple-element.150.refs_0_, bf16[2,4,64,128]{3,2,1,0:T(8,128)(2,1)} %copy-done.15, ...), custom_call_target="tpu_custom_call", output_to_operand_aliasing={{}: (34, {})} | custom-call | flops 4294967296 | bytes 14680064 | tf_op jit(solution)/shard_map/third/pallas_call | solution.py:223
  (291 shorter events, 136.1 us)
Async XLA Ops:
  72.2 25.5 %collective-permute-start.25 = (bf16[2,8,128,128]{3,2,1,0:T(8,128)(2,1)}, bf16[2,8,128,128]{3,2,1,0:T(8,128)(2,1)S(1)}, u32[]{:S(2)}, u32[]{:S(2)}) collective-permute-start(bf16[2,8,128,128]{3,2,1,0:T(8,128)(2,1)} %get-tuple-element.166), channel_id=1, source_target_pairs={{0,2},{1,3},{2,0},{3,1},{4,6},{5,7},{6,4},{7,5},{8,10},{9,11},{10,... | collective-permute-start | bytes 1572872 | tf_op jit(solution)/shard_map/ppermute | solution.py:257
  72.9 24.9 %collective-permute-start.26 = (bf16[2,8,128,128]{3,2,1,0:T(8,128)(2,1)}, bf16[2,8,128,128]{3,2,1,0:T(8,128)(2,1)S(1)}, u32[]{:S(2)}, u32[]{:S(2)}) collective-permute-start(bf16[2,8,128,128]{3,2,1,0:T(8,128)(2,1)} %get-tuple-element.168), channel_id=1, source_target_pairs={{0,3},{1,2},{2,1},{3,0},{4,7},{5,6},{6,5},{7,4},{8,11},{9,10},{10,... | collective-permute-start | bytes 1572872 | tf_op jit(solution)/shard_map/ppermute | solution.py:257
  92.8 22.7 %collective-permute-start.21 = (bf16[2,4,64,128]{3,2,1,0:T(8,128)(2,1)}, bf16[2,4,64,128]{3,2,1,0:T(8,128)(2,1)S(1)}, u32[]{:S(2)}, u32[]{:S(2)}) collective-permute-start(bf16[2,4,64,128]{3,2,1,0:T(8,128)(2,1)} %get-tuple-element.157), channel_id=1, source_target_pairs={{0,12},{4,8},{8,4},{12,0},{16,28},{20,24},{24,20},{28,16},{1,13},{... | collective-permute-start | bytes 393224 | tf_op jit(solution)/shard_map/ppermute | solution.py:257
  115.5 35.6 %collective-permute-start.35 = (bf16[2,20,128,128]{3,2,1,0:T(8,128)(2,1)}, bf16[2,20,128,128]{3,2,1,0:T(8,128)(2,1)S(1)}, u32[]{:S(2)}, u32[]{:S(2)}) collective-permute-start(bf16[2,20,128,128]{3,2,1,0:T(8,128)(2,1)} %get-tuple-element.193), channel_id=1, source_target_pairs={{0,2},{1,3},{2,0},{3,1},{4,6},{5,7},{6,4},{7,5},{8,10},{9,11},{10,... | collective-permute-start | bytes 3932168 | tf_op jit(solution)/shard_map/ppermute | solution.py:257
  121.4 29.8 %collective-permute-start.34 = (bf16[2,20,128,128]{3,2,1,0:T(8,128)(2,1)}, bf16[2,20,128,128]{3,2,1,0:T(8,128)(2,1)S(1)}, u32[]{:S(2)}, u32[]{:S(2)}) collective-permute-start(bf16[2,20,128,128]{3,2,1,0:T(8,128)(2,1)} %get-tuple-element.191), channel_id=1, source_target_pairs={{0,1},{1,0},{2,3},{3,2},{4,5},{5,4},{6,7},{7,6},{8,9},{9,8},{10,11... | collective-permute-start | bytes 3932168 | tf_op jit(solution)/shard_map/ppermute | solution.py:257
  131.6 19.5 %collective-permute-start.31 = (bf16[2,8,64,128]{3,2,1,0:T(8,128)(2,1)S(1)}, bf16[2,8,64,128]{3,2,1,0:T(8,128)(2,1)S(1)}, u32[]{:S(2)}, u32[]{:S(2)}) collective-permute-start(bf16[2,8,64,128]{3,2,1,0:T(8,128)(2,1)S(1)} %copy-done.63), channel_id=1, source_target_pairs={{0,12},{4,8},{8,4},{12,0},{16,28},{20,24},{24,20},{28,16},{1,13},{... | collective-permute-start | bytes 786440 | tf_op jit(solution)/shard_map/ppermute | solution.py:257
  151.2 31.6 %collective-permute-start.44 = (bf16[2,32,128,128]{3,2,1,0:T(8,128)(2,1)}, bf16[2,32,128,128]{3,2,1,0:T(8,128)(2,1)}, u32[]{:S(2)}, u32[]{:S(2)}) collective-permute-start(bf16[2,32,128,128]{3,2,1,0:T(8,128)(2,1)} %get-tuple-element.218), channel_id=1, source_target_pairs={{0,1},{1,0},{2,3},{3,2},{4,5},{5,4},{6,7},{7,6},{8,9},{9,8},{10,11... | collective-permute-start | bytes 6291464 | tf_op jit(solution)/shard_map/ppermute | solution.py:257
  151.3 30.5 %collective-permute-start.36 = (bf16[2,20,128,128]{3,2,1,0:T(8,128)(2,1)S(1)}, bf16[2,20,128,128]{3,2,1,0:T(8,128)(2,1)S(1)}, u32[]{:S(2)}, u32[]{:S(2)}) collective-permute-start(bf16[2,20,128,128]{3,2,1,0:T(8,128)(2,1)S(1)} %copy-done.50), channel_id=1, source_target_pairs={{0,3},{1,2},{2,1},{3,0},{4,7},{5,6},{6,5},{7,4},{8,11},{9,10},{10,... | collective-permute-start | bytes 3932168 | tf_op jit(solution)/shard_map/ppermute | solution.py:257
  181.8 94.6 %collective-permute-start.45 = (bf16[2,32,128,128]{3,2,1,0:T(8,128)(2,1)}, bf16[2,32,128,128]{3,2,1,0:T(8,128)(2,1)}, u32[]{:S(2)}, u32[]{:S(2)}) collective-permute-start(bf16[2,32,128,128]{3,2,1,0:T(8,128)(2,1)} %get-tuple-element.220), channel_id=1, source_target_pairs={{0,2},{1,3},{2,0},{3,1},{4,6},{5,7},{6,4},{7,5},{8,10},{9,11},{10,... | collective-permute-start | bytes 6291464 | tf_op jit(solution)/shard_map/ppermute | solution.py:257
  182.7 93.7 %collective-permute-start.46 = (bf16[2,32,128,128]{3,2,1,0:T(8,128)(2,1)}, bf16[2,32,128,128]{3,2,1,0:T(8,128)(2,1)}, u32[]{:S(2)}, u32[]{:S(2)}) collective-permute-start(bf16[2,32,128,128]{3,2,1,0:T(8,128)(2,1)} %get-tuple-element.222), channel_id=1, source_target_pairs={{0,3},{1,2},{2,1},{3,0},{4,7},{5,6},{6,5},{7,4},{8,11},{9,10},{10,... | collective-permute-start | bytes 6291464 | tf_op jit(solution)/shard_map/ppermute | solution.py:257
  194.4 51.0 %collective-permute-start.38 = (bf16[2,20,64,128]{3,2,1,0:T(8,128)(2,1)}, bf16[2,20,64,128]{3,2,1,0:T(8,128)(2,1)S(1)}, u32[]{:S(2)}, u32[]{:S(2)}) collective-permute-start(bf16[2,20,64,128]{3,2,1,0:T(8,128)(2,1)} %get-tuple-element.201), channel_id=1, source_target_pairs={{0,16},{4,20},{8,24},{12,28},{16,0},{20,4},{24,8},{28,12},{1,17},{... | collective-permute-start | bytes 1966088 | tf_op jit(solution)/shard_map/ppermute | solution.py:257
  201.5 58.7 %collective-permute-start.40 = (bf16[2,20,64,128]{3,2,1,0:T(8,128)(2,1)}, bf16[2,20,64,128]{3,2,1,0:T(8,128)(2,1)S(1)}, u32[]{:S(2)}, u32[]{:S(2)}) collective-permute-start(bf16[2,20,64,128]{3,2,1,0:T(8,128)(2,1)} %get-tuple-element.205), channel_id=1, source_target_pairs={{0,20},{4,16},{8,28},{12,24},{16,4},{20,0},{24,12},{28,8},{1,21},{... | collective-permute-start | bytes 1966088 | tf_op jit(solution)/shard_map/ppermute | solution.py:257
  202.6 57.6 %collective-permute-start.37 = (bf16[2,20,64,128]{3,2,1,0:T(8,128)(2,1)}, bf16[2,20,64,128]{3,2,1,0:T(8,128)(2,1)S(1)}, u32[]{:S(2)}, u32[]{:S(2)}) collective-permute-start(bf16[2,20,64,128]{3,2,1,0:T(8,128)(2,1)} %get-tuple-element.198), channel_id=1, source_target_pairs={{0,4},{4,0},{8,12},{12,8},{16,20},{20,16},{24,28},{28,24},{1,5},{5... | collective-permute-start | bytes 1966088 | tf_op jit(solution)/shard_map/ppermute | solution.py:257
  245.4 27.8 %collective-permute-start.39 = (bf16[2,20,64,128]{3,2,1,0:T(8,128)(2,1)}, bf16[2,20,64,128]{3,2,1,0:T(8,128)(2,1)S(1)}, u32[]{:S(2)}, u32[]{:S(2)}) collective-permute-start(bf16[2,20,64,128]{3,2,1,0:T(8,128)(2,1)} %get-tuple-element.202), channel_id=1, source_target_pairs={{0,8},{4,12},{8,0},{12,4},{16,24},{20,28},{24,16},{28,20},{1,9},{5... | collective-permute-start | bytes 1966088 | tf_op jit(solution)/shard_map/ppermute | solution.py:257
  260.3 69.1 %collective-permute-start.41 = (bf16[2,20,64,128]{3,2,1,0:T(8,128)(2,1)}, bf16[2,20,64,128]{3,2,1,0:T(8,128)(2,1)S(1)}, u32[]{:S(2)}, u32[]{:S(2)}) collective-permute-start(bf16[2,20,64,128]{3,2,1,0:T(8,128)(2,1)} %get-tuple-element.206), channel_id=1, source_target_pairs={{0,12},{4,8},{8,4},{12,0},{16,28},{20,24},{24,20},{28,16},{1,13},{... | collective-permute-start | bytes 1966088 | tf_op jit(solution)/shard_map/ppermute | solution.py:257
  260.3 33.1 %collective-permute-start.42 = (bf16[2,20,64,128]{3,2,1,0:T(8,128)(2,1)}, bf16[2,20,64,128]{3,2,1,0:T(8,128)(2,1)S(1)}, u32[]{:S(2)}, u32[]{:S(2)}) collective-permute-start(bf16[2,20,64,128]{3,2,1,0:T(8,128)(2,1)} %get-tuple-element.208), channel_id=1, source_target_pairs={{0,24},{4,28},{8,16},{12,20},{16,8},{20,12},{24,0},{28,4},{1,25},{... | collective-permute-start | bytes 1966088 | tf_op jit(solution)/shard_map/ppermute | solution.py:257
  273.3 38.4 %collective-permute-start.43 = (bf16[2,20,64,128]{3,2,1,0:T(8,128)(2,1)}, bf16[2,20,64,128]{3,2,1,0:T(8,128)(2,1)S(1)}, u32[]{:S(2)}, u32[]{:S(2)}) collective-permute-start(bf16[2,20,64,128]{3,2,1,0:T(8,128)(2,1)} %get-tuple-element.210), channel_id=1, source_target_pairs={{0,28},{4,24},{8,20},{12,16},{16,12},{20,8},{24,4},{28,0},{1,29},{... | collective-permute-start | bytes 1966088 | tf_op jit(solution)/shard_map/ppermute | solution.py:257
  293.4 45.2 %collective-permute-start.55 = (bf16[2,32,16,128]{3,2,1,0:T(8,128)(2,1)}, bf16[2,32,16,128]{3,2,1,0:T(8,128)(2,1)S(1)}, u32[]{:S(2)}, u32[]{:S(2)}) collective-permute-start(bf16[2,32,16,128]{3,2,1,0:T(8,128)(2,1)} %get-tuple-element.249), channel_id=1, source_target_pairs={{0,16},{4,20},{8,24},{12,28},{16,0},{20,4},{24,8},{28,12},{1,17},{... | collective-permute-start | bytes 786440 | tf_op jit(solution)/shard_map/ppermute | solution.py:257
  311.6 32.0 %collective-permute-start.64 = (bf16[2,32,16,128]{3,2,1,0:T(8,128)(2,1)}, bf16[2,32,16,128]{3,2,1,0:T(8,128)(2,1)S(1)}, u32[]{:S(2)}, u32[]{:S(2)}) collective-permute-start(bf16[2,32,16,128]{3,2,1,0:T(8,128)(2,1)} %get-tuple-element.267), channel_id=1, source_target_pairs={{0,20},{4,16},{8,28},{12,24},{16,4},{20,0},{24,12},{28,8},{1,21},{... | collective-permute-start | bytes 786440 | tf_op jit(solution)/shard_map/ppermute | solution.py:257
  343.6 22.0 %collective-permute-start.65 = (bf16[2,32,16,128]{3,2,1,0:T(8,128)(2,1)}, bf16[2,32,16,128]{3,2,1,0:T(8,128)(2,1)S(1)}, u32[]{:S(2)}, u32[]{:S(2)}) collective-permute-start(bf16[2,32,16,128]{3,2,1,0:T(8,128)(2,1)} %get-tuple-element.268), channel_id=1, source_target_pairs={{0,12},{4,8},{8,4},{12,0},{16,28},{20,24},{24,20},{28,16},{1,13},{... | collective-permute-start | bytes 786440 | tf_op jit(solution)/shard_map/ppermute | solution.py:257
  343.6 22.4 %collective-permute-start.48 = (bf16[2,32,16,128]{3,2,1,0:T(8,128)(2,1)}, bf16[2,32,16,128]{3,2,1,0:T(8,128)(2,1)S(1)}, u32[]{:S(2)}, u32[]{:S(2)}) collective-permute-start(bf16[2,32,16,128]{3,2,1,0:T(8,128)(2,1)} %get-tuple-element.233), channel_id=1, source_target_pairs={{0,24},{4,28},{8,16},{12,20},{16,8},{20,12},{24,0},{28,4},{1,25},{... | collective-permute-start | bytes 786440 | tf_op jit(solution)/shard_map/ppermute | solution.py:257
  366.1 25.1 %collective-permute-start.49 = (bf16[2,32,16,128]{3,2,1,0:T(8,128)(2,1)}, bf16[2,32,16,128]{3,2,1,0:T(8,128)(2,1)S(1)}, u32[]{:S(2)}, u32[]{:S(2)}) collective-permute-start(bf16[2,32,16,128]{3,2,1,0:T(8,128)(2,1)} %get-tuple-element.234), channel_id=1, source_target_pairs={{0,16},{4,20},{8,24},{12,28},{16,0},{20,4},{24,8},{28,12},{1,17},{... | collective-permute-start | bytes 786440 | tf_op jit(solution)/shard_map/ppermute | solution.py:257
  366.6 31.3 %collective-permute-start.58 = (bf16[2,32,16,128]{3,2,1,0:T(8,128)(2,1)}, bf16[2,32,16,128]{3,2,1,0:T(8,128)(2,1)S(1)}, u32[]{:S(2)}, u32[]{:S(2)}) collective-permute-start(bf16[2,32,16,128]{3,2,1,0:T(8,128)(2,1)} %get-tuple-element.252), channel_id=1, source_target_pairs={{0,20},{4,16},{8,28},{12,24},{16,4},{20,0},{24,12},{28,8},{1,21},{... | collective-permute-start | bytes 786440 | tf_op jit(solution)/shard_map/ppermute | solution.py:257
  373.7 24.2 %collective-permute-start.67 = (bf16[2,32,16,128]{3,2,1,0:T(8,128)(2,1)}, bf16[2,32,16,128]{3,2,1,0:T(8,128)(2,1)S(1)}, u32[]{:S(2)}, u32[]{:S(2)}) collective-permute-start(bf16[2,32,16,128]{3,2,1,0:T(8,128)(2,1)} %get-tuple-element.270), channel_id=1, source_target_pairs={{0,24},{4,28},{8,16},{12,20},{16,8},{20,12},{24,0},{28,4},{1,25},{... | collective-permute-start | bytes 786440 | tf_op jit(solution)/shard_map/ppermute | solution.py:257
  397.9 24.1 %collective-permute-start.68 = (bf16[2,32,16,128]{3,2,1,0:T(8,128)(2,1)}, bf16[2,32,16,128]{3,2,1,0:T(8,128)(2,1)S(1)}, u32[]{:S(2)}, u32[]{:S(2)}) collective-permute-start(bf16[2,32,16,128]{3,2,1,0:T(8,128)(2,1)} %get-tuple-element.271), channel_id=1, source_target_pairs={{0,16},{4,20},{8,24},{12,28},{16,0},{20,4},{24,8},{28,12},{1,17},{... | collective-permute-start | bytes 786440 | tf_op jit(solution)/shard_map/ppermute | solution.py:257
  422.0 31.1 %collective-permute-start.52 = (bf16[2,32,16,128]{3,2,1,0:T(8,128)(2,1)}, bf16[2,32,16,128]{3,2,1,0:T(8,128)(2,1)S(1)}, u32[]{:S(2)}, u32[]{:S(2)}) collective-permute-start(bf16[2,32,16,128]{3,2,1,0:T(8,128)(2,1)} %get-tuple-element.237), channel_id=1, source_target_pairs={{0,20},{4,16},{8,28},{12,24},{16,4},{20,0},{24,12},{28,8},{1,21},{... | collective-permute-start | bytes 786440 | tf_op jit(solution)/shard_map/ppermute | solution.py:257
  428.9 24.2 %collective-permute-start.61 = (bf16[2,32,16,128]{3,2,1,0:T(8,128)(2,1)}, bf16[2,32,16,128]{3,2,1,0:T(8,128)(2,1)S(1)}, u32[]{:S(2)}, u32[]{:S(2)}) collective-permute-start(bf16[2,32,16,128]{3,2,1,0:T(8,128)(2,1)} %get-tuple-element.255), channel_id=1, source_target_pairs={{0,24},{4,28},{8,16},{12,20},{16,8},{20,12},{24,0},{28,4},{1,25},{... | collective-permute-start | bytes 786440 | tf_op jit(solution)/shard_map/ppermute | solution.py:257
  431.0 40.7 %collective-permute-start.70 = (bf16[2,32,16,128]{3,2,1,0:T(8,128)(2,1)}, bf16[2,32,16,128]{3,2,1,0:T(8,128)(2,1)S(1)}, u32[]{:S(2)}, u32[]{:S(2)}) collective-permute-start(bf16[2,32,16,128]{3,2,1,0:T(8,128)(2,1)} %get-tuple-element.273), channel_id=1, source_target_pairs={{0,28},{4,24},{8,20},{12,16},{16,12},{20,8},{24,4},{28,0},{1,29},{... | collective-permute-start | bytes 786440 | tf_op jit(solution)/shard_map/ppermute | solution.py:257
  453.1 19.6 %collective-permute-start.53 = (bf16[2,32,16,128]{3,2,1,0:T(8,128)(2,1)}, bf16[2,32,16,128]{3,2,1,0:T(8,128)(2,1)S(1)}, u32[]{:S(2)}, u32[]{:S(2)}) collective-permute-start(bf16[2,32,16,128]{3,2,1,0:T(8,128)(2,1)} %get-tuple-element.238), channel_id=1, source_target_pairs={{0,12},{4,8},{8,4},{12,0},{16,28},{20,24},{24,20},{28,16},{1,13},{... | collective-permute-start | bytes 786440 | tf_op jit(solution)/shard_map/ppermute | solution.py:257
  453.1 28.9 %collective-permute-start.62 = (bf16[2,32,16,128]{3,2,1,0:T(8,128)(2,1)}, bf16[2,32,16,128]{3,2,1,0:T(8,128)(2,1)S(1)}, u32[]{:S(2)}, u32[]{:S(2)}) collective-permute-start(bf16[2,32,16,128]{3,2,1,0:T(8,128)(2,1)} %get-tuple-element.256), channel_id=1, source_target_pairs={{0,16},{4,20},{8,24},{12,28},{16,0},{20,4},{24,8},{28,12},{1,17},{... | collective-permute-start | bytes 786440 | tf_op jit(solution)/shard_map/ppermute | solution.py:257
  471.7 22.0 %collective-permute-start.71 = (bf16[2,32,16,128]{3,2,1,0:T(8,128)(2,1)}, bf16[2,32,16,128]{3,2,1,0:T(8,128)(2,1)S(1)}, u32[]{:S(2)}, u32[]{:S(2)}) collective-permute-start(bf16[2,32,16,128]{3,2,1,0:T(8,128)(2,1)} %get-tuple-element.274), channel_id=1, source_target_pairs={{0,20},{4,16},{8,28},{12,24},{16,4},{20,0},{24,12},{28,8},{1,21},{... | collective-permute-start | bytes 786440 | tf_op jit(solution)/shard_map/ppermute | solution.py:257
  472.7 22.8 %collective-permute-start.54 = (bf16[2,32,16,128]{3,2,1,0:T(8,128)(2,1)S(1)}, bf16[2,32,16,128]{3,2,1,0:T(8,128)(2,1)S(1)}, u32[]{:S(2)}, u32[]{:S(2)}) collective-permute-start(bf16[2,32,16,128]{3,2,1,0:T(8,128)(2,1)S(1)} %copy-done.60), channel_id=1, source_target_pairs={{0,4},{4,0},{8,12},{12,8},{16,20},{20,16},{24,28},{28,24},{1,5},{5... | collective-permute-start | bytes 786440 | tf_op jit(solution)/shard_map/ppermute | solution.py:257
  (114 other events, 3305.8 us)

commit v2 on v1

--- a/solution.py
+++ b/solution.py
@@ -7,6 +7,12 @@
 from jax.experimental.pallas import tpu as pltpu
 from jax.sharding import PartitionSpec as P
 
+COUNTS = (3, 5, 8, 16)
+DEPTH = 5
+WAIT = 3
+FIRST = 5
+SECOND = 6
+BLOCK = 16
 VMEM_BYTES = 56 * 1024 * 1024
 
 
@@ -52,56 +58,95 @@
     return block
 
 
-def first_kernel(place, mixing, elem, *outs):
+def first_kernel(mixing, elem, out):
     width = elem.shape[-1]
     count, local_j = elem.shape[1], elem.shape[2]
-    cols = outs[0].shape[-1]
+    cols = out.shape[-1]
     left = jnp.concatenate(
         [elem[0].reshape(count * local_j, width), elem[1].reshape(count * local_j, width)], axis=1
     )
-    for t, out in enumerate(outs):
-        start = pl.multiple_of((place[1] ^ t) * cols, cols)
+    for d in range(out.shape[0]):
         right = jnp.concatenate(
-            [mixing[pl.ds(start, cols), :], mixing[pl.ds(width + start, cols), :]], axis=0
+            [mixing[s * width + d * cols : s * width + (d + 1) * cols, :] for s in range(2)], axis=0
         )
         res = lax.dot_general(
             left, right, (((1,), (1,)), ((), ())), preferred_element_type=jnp.float32
         ).astype(jnp.bfloat16)
         for s in range(2):
-            out[s] = res[:, s * cols : (s + 1) * cols].reshape(count, local_j, cols)
-
-
-def contract_first(mixing, elemental, place, offset, count, col_count):
+            out[d, s] = res[:, s * cols : (s + 1) * cols].reshape(count, local_j, cols)
+
+
+def contract_first(mixing, elemental, offset, count, col_count):
     _, _, local_j, width = elemental.shape
     cols = width // col_count
     step = count if offset == 0 else min(offset, count)
     while count % step or offset % step or step > 4:
         step -= 1
-    out_shape = jax.ShapeDtypeStruct((2, count, local_j, cols), jnp.bfloat16)
     return pl.pallas_call(
         first_kernel,
         name="first",
         grid=(count // step,),
         in_specs=[
-            pl.BlockSpec(memory_space=pltpu.SMEM),
             pl.BlockSpec(mixing.shape, lambda n: (0, 0)),
             pl.BlockSpec((2, step, local_j, width), lambda n: (0, offset // step + n, 0, 0)),
         ],
-        out_specs=[pl.BlockSpec((2, step, local_j, cols), lambda n: (0, n, 0, 0))] * col_count,
-        out_shape=[out_shape] * col_count,
+        out_specs=pl.BlockSpec((col_count, 2, step, local_j, cols), lambda n: (0, 0, n, 0, 0)),
+        out_shape=jax.ShapeDtypeStruct((col_count, 2, count, local_j, cols), jnp.bfloat16),
         compiler_params=pltpu.CompilerParams(vmem_limit_bytes=VMEM_BYTES),
         cost_estimate=pl.CostEstimate(
             flops=8 * count * local_j * width * width,
             bytes_accessed=8 * count * local_j * width + 8 * width * width,
             transcendentals=0,
         ),
-    )(place, mixing, elemental)
-
-
-def second_kernel(col_count, row_count, splits, place, mixing, *refs):
-    blocks, outs, (ordered, right) = refs[:col_count], refs[col_count:-2], refs[-2:]
+    )(mixing, elemental)
+
+
+def gathered_kernel(place, mixing, elem, out):
+    width, cols = mixing.shape[0] // 2, out.shape[-1]
+    col_count, _, count, local_j, _ = elem.shape
+    start = pl.multiple_of(place[1] * cols, cols)
+    right = jnp.concatenate(
+        [mixing[pl.ds(start, cols), :], mixing[pl.ds(width + start, cols), :]], axis=0
+    )
+    for d in range(col_count):
+        left = jnp.concatenate(
+            [elem[d, r].reshape(count * local_j, width) for r in range(2)], axis=1
+        )
+        res = lax.dot_general(
+            left, right, (((1,), (1,)), ((), ())), preferred_element_type=jnp.float32
+        ).astype(jnp.bfloat16)
+        for s in range(2):
+            out[d, s] = res[:, s * cols : (s + 1) * cols].reshape(count, local_j, cols)
+
+
+def contract_gathered(mixing, gathered, place):
+    col_count, _, count, local_j, width = gathered.shape
+    cols = width // col_count
+    step = 2 if count % 2 == 0 else 1
+    return pl.pallas_call(
+        gathered_kernel,
+        name="gathered",
+        grid=(count // step,),
+        in_specs=[
+            pl.BlockSpec(memory_space=pltpu.SMEM),
+            pl.BlockSpec(mixing.shape, lambda n: (0, 0)),
+            pl.BlockSpec((col_count, 2, step, local_j, width), lambda n: (0, 0, n, 0, 0)),
+        ],
+        out_specs=pl.BlockSpec((col_count, 2, step, local_j, cols), lambda n: (0, 0, n, 0, 0)),
+        out_shape=jax.ShapeDtypeStruct((col_count, 2, count, local_j, cols), jnp.bfloat16),
+        compiler_params=pltpu.CompilerParams(vmem_limit_bytes=VMEM_BYTES),
+        cost_estimate=pl.CostEstimate(
+            flops=8 * count * local_j * width * width,
+            bytes_accessed=8 * count * local_j * width + 8 * width * width,
+            transcendentals=0,
+        ),
+    )(place, mixing, gathered)
+
+
+def second_kernel(row_count, parts, place, mixing, block, *refs):
+    outs, (ordered, right) = refs[:-2], refs[-2:]
     width = mixing.shape[0] // 2
-    _, count, local_j, cols = blocks[0].shape
+    col_count, _, count, local_j, cols = block.shape
     local_b = width // row_count
 
     @pl.when(pl.program_id(0) == 0)
@@ -113,45 +158,43 @@
                     pl.ds(s * width + start, local_b), :
                 ]
 
-    for t, block in enumerate(blocks):
-        start = pl.multiple_of((place[1] ^ t) * local_j, local_j)
+    for d in range(col_count):
         for r in range(2):
+            row = r * width + d * local_j
             for i in range(count):
-                right[pl.ds(r * width + start, local_j), i * cols : (i + 1) * cols] = block[r, i]
+                right[row : row + local_j, i * cols : (i + 1) * cols] = block[d, r, i]
     res = jnp.dot(ordered[...], right[...], preferred_element_type=jnp.float32)
     res = res.astype(jnp.bfloat16)
-    part = local_b // splits
-    for u in range(splits):
+    for u, part in enumerate(parts):
         for t in range(row_count):
             for s in range(2):
-                row = (2 * t + s) * local_b + u * part
+                row = (2 * t + s) * local_b + sum(parts[:u])
                 for i in range(count):
                     outs[u * row_count + t][s, i] = res[
                         row : row + part, i * cols : (i + 1) * cols
                     ]
 
 
-def contract_second(mixing, blocks, place, row_count, splits):
-    col_count = len(blocks)
-    _, count, local_j, cols = blocks[0].shape
+def contract_second(mixing, block, place, row_count, parts):
+    col_count, _, count, local_j, cols = block.shape
     width = mixing.shape[0] // 2
-    part = width // row_count // splits
     step = min(count, 4)
     while count % step:
         step -= 1
-    out_shape = jax.ShapeDtypeStruct((2, count, part, cols), jnp.bfloat16)
+    shapes = [(2, count, part, cols) for part in parts for _ in range(row_count)]
     outs = pl.pallas_call(
-        functools.partial(second_kernel, col_count, row_count, splits),
+        functools.partial(second_kernel, row_count, parts),
         name="second",
         grid=(count // step,),
         in_specs=[
             pl.BlockSpec(memory_space=pltpu.SMEM),
             pl.BlockSpec(mixing.shape, lambda n: (0, 0)),
         ]
-        + [pl.BlockSpec((2, step, local_j, cols), lambda n: (0, n, 0, 0))] * col_count,
-        out_specs=[pl.BlockSpec((2, step, part, cols), lambda n: (0, n, 0, 0))]
-        * (row_count * splits),
-        out_shape=[out_shape] * (row_count * splits),
+        + [pl.BlockSpec((col_count, 2, step, local_j, cols), lambda n: (0, 0, n, 0, 0))],
+        out_specs=[
+            pl.BlockSpec((2, step) + shape[2:], lambda n: (0, n, 0, 0)) for shape in shapes
+        ],
+        out_shape=[jax.ShapeDtypeStruct(shape, jnp.bfloat16) for shape in shapes],
         scratch_shapes=[
             pltpu.VMEM(mixing.shape, jnp.bfloat16),
             pltpu.VMEM((2 * width, step * cols), jnp.bfloat16),
@@ -162,8 +205,8 @@
             bytes_accessed=8 * count * cols * width + 8 * width * width,
             transcendentals=0,
         ),
-    )(place, mixing, *blocks)
-    return [outs[u * row_count : (u + 1) * row_count] for u in range(splits)]
+    )(place, mixing, block)
+    return [outs[u * row_count : (u + 1) * row_count] for u in range(len(parts))]
 
 
 def third_kernel(row_count, offsets, rows, aliased, place, mixing, *refs):
@@ -198,19 +241,16 @@
             result[pl.ds(b + n, depth, stride=rows), :] = res[:, n * cols : (n + 1) * cols]
 
 
-def contract_third(mixing, chunks, place, offsets, index, splits, previous):
+def contract_third(mixing, chunks, places, place, offsets, index, local_b, previous):
     row_count = len(chunks[0])
-    depth = mixing.shape[0]
-    cols = chunks[0][0].shape[-1]
-    part = chunks[-1][0].shape[2]
-    rows = 8
+    depth, cols = mixing.shape[0], chunks[0][0].shape[-1]
+    part, rows = BLOCK, 8
     in_specs = [
         pl.BlockSpec(memory_space=pltpu.SMEM),
         pl.BlockSpec(mixing.shape, lambda n: (0, 0)),
     ]
     operands = [place, mixing]
-    for q, chunk in enumerate(chunks):
-        where = index if chunk[0].shape[2] != part else 0
+    for chunk, where in zip(chunks, places):
         for block in chunk:
             shape = (2, block.shape[1], part, cols)
             in_specs.append(pl.BlockSpec(shape, lambda n, where=where: (0, 0, where, 0)))
@@ -226,7 +266,7 @@
         grid=(part // rows,),
         in_specs=in_specs,
         out_specs=pl.BlockSpec((depth, rows, cols), lambda n: (0, index * (part // rows) + n, 0)),
-        out_shape=jax.ShapeDtypeStruct((depth, part * splits, cols), jnp.float32),
+        out_shape=jax.ShapeDtypeStruct((depth, local_b, cols), jnp.float32),
         scratch_shapes=[pltpu.VMEM((depth, part, cols), jnp.float32)],
         input_output_aliases=aliases,
         compiler_params=pltpu.CompilerParams(vmem_limit_bytes=VMEM_BYTES),
@@ -251,9 +291,9 @@
         self.depth = depth
         self.results = []
 
-    def send(self, block, bit):
-        if len(self.results) >= self.depth:
-            block, _ = lax.optimization_barrier((block, self.results[-self.depth]))
+    def send(self, block, bit, *others):
+        before = self.results[-self.depth :][: len(self.results) >= self.depth]
+        block = after(block, *before, *others)
         result = lax.ppermute(block, self.axis, flip(lax.axis_size(self.axis), bit))
         self.results.append(result)
         return result
@@ -276,7 +316,7 @@
     )
     mixing = build_mixing(chosen.reshape(2, width, width))
 
-    if cols % 128 or local_b % 16 or local_i % 16 or not is_power_of_two(row_count * col_count):
+    if cols % 128 or local_b % BLOCK or local_i % 16 or not is_power_of_two(row_count * col_count):
         mixing = mixing.reshape(2, width, 2, width)
         first = jnp.einsum("scrk,rijk->sijc", mixing, elemental, preferred_element_type=jnp.float32)
         first = lax.all_to_all(first.astype(jnp.bfloat16), "col", 3, 2, tiled=True)
@@ -284,37 +324,59 @@
         second = lax.all_to_all(second.astype(jnp.bfloat16), "row", 1, 2, tiled=True)
         return jnp.einsum("sari,rbic->sabc", mixing, second, preferred_element_type=jnp.float32)
 
-    counts = [local_i // 16, local_i // 8, local_i * 5 // 16]
+    counts = [local_i * n // sum(COUNTS) for n in COUNTS[:-1]]
     counts.append(local_i - sum(counts))
     offsets = [sum(counts[:q]) for q in range(len(counts))]
-    splits = local_b // 16
     half = row_count // 2
     order = [half] + [t for n in range(1, half) for t in (n, half + n)]
-    col_lane, row_lane = Lane("col", 2), Lane("row", 3)
+    order[-2:] = order[:-3:-1]
+    row_lane = Lane("row", DEPTH)
     last = len(counts) - 1
-    firsts, chunks, tails = {}, [], []
-
-    def start(q, token, wait):
-        blocks = contract_first(mixing, elemental, after(place, token), offsets[q], counts[q], col_count)
-        blocks = after(blocks, *wait)
-        firsts[q] = [blocks[0]] + [col_lane.send(blocks[t], t) for t in range(1, col_count)]
-
-    start(0, mixing, [])
-    start(1, mixing, [])
-    for q in range(len(counts)):
+    tail = [BLOCK] * (local_b // BLOCK)
+    chunks, tails = [], []
+
+    def contract(q, *others):
+        return contract_first(
+            mixing, after(elemental, *others), offsets[q], counts[q], col_count
+        )
+
+    def send_first(block, *others):
+        return lax.all_to_all(after(block, *others), "col", 0, 0, tiled=True)
+
+    def send_second(part, waits):
+        arrived = {0: part[0]}
+        for n, t in enumerate(order):
+            arrived[t] = row_lane.send(part[t], t, *waits.get(n, []))
+        return [arrived[t] for t in range(row_count)]
+
+    raw = lax.all_gather(elemental[:, : counts[0]], "col")
+    following = contract(1)
+    swapped = contract_gathered(mixing, raw, after(place, following))
+    parts = contract_second(mixing, swapped, place, row_count, [local_b])
+    swapped = send_first(following, swapped)
+    for q in range(last):
+        waits = {}
+        if q + 2 <= last:
+            following = contract(q + 2, parts[0][0])
+            waits[FIRST] = [following]
+        now = parts[0]
         parts = contract_second(
-            mixing, firsts[q], place, row_count, splits if q == last else 1
-        )
-        for part in parts:
-            arrived = {0: part[0]}
-            for t in order:
-                arrived[t] = row_lane.send(part[t], t)
-            (tails if q == last else chunks).append([arrived[t] for t in range(row_count)])
+            mixing, swapped, place, row_count, tail if q + 1 == last else [local_b]
+        )
+        waits[SECOND] = [parts[0][0]]
+        chunks.append(send_second(now, waits))
         if q + 2 <= last:
-            start(q + 2, parts[0][0], [arrived[t] for t in order])
-    result = None
-    for u, tail in enumerate(tails):
-        result = contract_third(mixing, chunks + [tail], place, offsets, u, splits, result)
+            held = [chunks[q][t] for t in order[:WAIT]]
+            swapped = send_first(following, swapped, *held)
+    for part in parts:
+        tails.append(send_second(part, {}))
+    result, index = None, 0
+    for part, blocks in zip(tail, tails):
+        for n in range(part // BLOCK):
+            result = contract_third(
+                mixing, chunks + [blocks], [index] * last + [n], place, offsets, index, local_b, result
+            )
+            index += 1
     return result.reshape(2, width, local_b, cols)
 
 

time: 529 us -> 508 us (0.960)
  waiting for transfers between devices: 247 us -> 165 us
  starting transfers between devices: 153 us -> 195 us
  between operations: 1.86 us -> 14.8 us
    ppermute x61 -> x49, waiting for transfers between devices: 219 us -> 121 us  [send(): result = lax.ppermute(block, self.axis, flip(lax.axis_size(self.axis), bit))]
    ppermute x61 -> x49, starting transfers between devices: 133 us -> 161 us  [send(): result = lax.ppermute(block, self.axis, flip(lax.axis_size(self.axis), bit))]
    all_to_all x0 -> x3, starting transfers between devices: none -> 14.4 us  [send_first(): return lax.all_to_all(after(block, *others), 'col', 0, 0, tiled=True)]
    all_to_all x0 -> x3, waiting for transfers between devices: none -> 14.1 us  [send_first(): return lax.all_to_all(after(block, *others), 'col', 0, 0, tiled=True)]
    pallas_call x4 -> x5, Pallas kernels: 37.7 us -> 45.4 us  [the longest x4 38.8 us: contract_second(): pl.pallas_call(functools.partial(second_kernel, row_count, parts), name='...]
    pallas_call x4 -> x3, Pallas kernels: 34.3 us -> 30.2 us  [contract_first(): pl.pallas_call(first_kernel, name='first', grid=(count // step,), in_spec...]
  transfers between devices with their start and end apart: 75 -> 67, of which waited for: 34 -> 31; matrix products, arithmetic and copies ran while one was open for 0% -> 1% of each run, Pallas kernels for 20% -> 20%
where the time goes in v2:
time: 508 us; the launch traced here: 507 us
  starting transfers between devices  195 us (38%)
  waiting for transfers between devices  165 us (32%)
  Pallas kernels  121 us (24%)
  between operations  14.8 us (3%)
  local copies, waits for them, and re-layouts  7.01 us (1%)
    ppermute x49, starting transfers between devices, send(): result = lax.ppermute(block, self.axis, flip(lax.axis_size(self.axis), bit))  161 us
    ppermute x49, waiting for transfers between devices, send(): result = lax.ppermute(block, self.axis, flip(lax.axis_size(self.axis), bit))  121 us
    pallas_call x4, Pallas kernels, contract_third(): pl.pallas_call(functools.partial(third_kernel, row_count, offsets, rows,...  45.9 us
    pallas_call x4, Pallas kernels, contract_second(): pl.pallas_call(functools.partial(second_kernel, row_count, parts), name='...  38.8 us
    pallas_call x3, Pallas kernels, contract_first(): pl.pallas_call(first_kernel, name='first', grid=(count // step,), in_spec...  30.2 us
    ppermute x13, waiting for transfers between devices, take_from_owner(): received = lax.ppermute(block, axis, flip(lax.axis_size(axis), bit))  29 us
    ppermute x13, starting transfers between devices, take_from_owner(): received = lax.ppermute(block, axis, flip(lax.axis_size(axis), bit))  19.4 us
    all_to_all x3, starting transfers between devices, send_first(): return lax.all_to_all(after(block, *others), 'col', 0, 0, tiled=True)  14.4 us
  transfers between devices with their start and end apart: 67, of which 31 were waited for; matrix products, arithmetic and copies ran while one was open for 1% of the time, Pallas kernels for 20%

profile of v2, /device:TPU:0, one launch (start us, length us, event | category | flops | bytes accessed | tf_op | source)
XLA Modules:
  0.0 506.6 jit_solution(974608707127270781)
XLA Ops:
  32.8 9.0 %collective-permute-done.6 = bf16[176,512]{1,0:T(8,128)(2,1)S(1)} collective-permute-done((bf16[176,512]{1,0:T(8,128)(2,1)S(1)}, bf16[176,512]{1,0:T(8,128)(2,1)S(1)}, u32[]{:S(2)}, u32[]{:S(2)}) %collective-permute-start.6) | collective-permute-done | bytes 180256 | tf_op jit(solution)/shard_map/ppermute | solution.py:28
  45.3 7.5 %collective-permute-done.7 = bf16[176,512]{1,0:T(8,128)(2,1)S(1)} collective-permute-done((bf16[176,512]{1,0:T(8,128)(2,1)S(1)}, bf16[176,512]{1,0:T(8,128)(2,1)S(1)}, u32[]{:S(2)}, u32[]{:S(2)}) %collective-permute-start.7) | collective-permute-done | bytes 180256 | tf_op jit(solution)/shard_map/ppermute | solution.py:28
  62.9 7.3 %first.3 = bf16[4,2,10,128,128]{4,3,2,1,0:T(8,128)(2,1)} custom-call(bf16[1024,1024]{1,0:T(8,128)(2,1)} %maximum_maximum_fusion.mixing, bf16[2,64,128,512]{3,2,1,0:T(8,128)(2,1)} %elem.3), custom_call_target="tpu_custom_call" | custom-call | flops 2684354560 | bytes 7340032 | tf_op jit(solution)/shard_map/first/pallas_call | solution.py:85
  70.3 6.5 %gathered.1.block = bf16[4,2,6,128,128]{4,3,2,1,0:T(8,128)(2,1)} custom-call(s32[2]{0:T(128)} %pad_add_fusion.place, bf16[1024,1024]{1,0:T(8,128)(2,1)} %maximum_maximum_fusion.mixing, bf16[4,2,6,128,512]{4,3,2,1,0:T(8,128)(2,1)} %bitcast.11), custom_call_target="tpu_custom_call" | custom-call | flops 1610612736 | bytes 5242880 | tf_op jit(solution)/shard_map/gathered/pallas_call | solution.py:126
  80.4 5.7 %second.4 = (bf16[2,6,64,128]{3,2,1,0:T(8,128)(2,1)}, bf16[2,6,64,128]{3,2,1,0:T(8,128)(2,1)}, bf16[2,6,64,128]{3,2,1,0:T(8,128)(2,1)}, bf16[2,6,64,128]{3,2,1,0...) custom-call(s32[2]{0:T(128)} %pad_add_fusion.place, ...), custom_call_target="tpu_custom_call" | custom-call | flops 1610612736 | bytes 5242880 | tf_op jit(solution)/shard_map/second/pallas_call | solution.py:185
  90.6 8.5 %first.4 = bf16[4,2,16,128,128]{4,3,2,1,0:T(8,128)(2,1)} custom-call(bf16[1024,1024]{1,0:T(8,128)(2,1)} %maximum_maximum_fusion.mixing, bf16[2,64,128,512]{3,2,1,0:T(8,128)(2,1)} %elem.3), custom_call_target="tpu_custom_call" | custom-call | flops 4294967296 | bytes 10485760 | tf_op jit(solution)/shard_map/first/pallas_call | solution.py:85
  121.6 7.6 %second.5 = (bf16[2,10,64,128]{3,2,1,0:T(8,128)(2,1)}, bf16[2,10,64,128]{3,2,1,0:T(8,128)(2,1)}, bf16[2,10,64,128]{3,2,1,0:T(8,128)(2,1)}, bf16[2,10,64,128]{3,2...) custom-call(s32[2]{0:T(128)} %pad_add_fusion.place, ...), custom_call_target="tpu_custom_call" | custom-call | flops 2684354560 | bytes 7340032 | tf_op jit(solution)/shard_map/second/pallas_call | solution.py:185
  135.4 14.4 %first.5 = bf16[4,2,32,128,128]{4,3,2,1,0:T(8,128)(2,1)} custom-call(bf16[1024,1024]{1,0:T(8,128)(2,1)} %maximum_maximum_fusion.mixing, bf16[2,64,128,512]{3,2,1,0:T(8,128)(2,1)} %elem.3), custom_call_target="tpu_custom_call" | custom-call | flops 8589934592 | bytes 18874368 | tf_op jit(solution)/shard_map/first/pallas_call | solution.py:85
  155.1 6.8 %collective-permute-done.24.refs_12_ = bf16[2,10,64,128]{3,2,1,0:T(8,128)(2,1)} collective-permute-done((bf16[2,10,64,128]{3,2,1,0:T(8,128)(2,1)}, bf16[2,10,64,128]{3,2,1,0:T(8,128)(2,1)}, u32[]{:S(2)}, u32[]{:S(2)}) %collective-permute-start.24) | collective-permute-done | bytes 327712 | tf_op jit(solution)/shard_map/ppermute | solution.py:297
  166.3 5.8 %all-to-all-start.2 = ((bf16[4,2,32,128,128]{4,3,2,1,0:T(8,128)(2,1)}), bf16[4,2,32,128,128]{4,3,2,1,0:T(8,128)(2,1)}, u32[]{:S(2)}, u32[]{:S(2)}) async-start(bf16[4,2,32,128,128]{4,3,2,1,0:T(8,128)(2,1)} %first.5), calls=%async_computation.2 | async-start | bytes 16777216 | tf_op jit(solution)/shard_map/all_to_all | solution.py:344
  176.0 9.2 %second.6 = (bf16[2,16,64,128]{3,2,1,0:T(8,128)(2,1)}, bf16[2,16,64,128]{3,2,1,0:T(8,128)(2,1)}, bf16[2,16,64,128]{3,2,1,0:T(8,128)(2,1)}, bf16[2,16,64,128]{3,2...) custom-call(s32[2]{0:T(128)} %pad_add_fusion.place, ...), custom_call_target="tpu_custom_call" | custom-call | flops 4294967296 | bytes 10485760 | tf_op jit(solution)/shard_map/second/pallas_call | solution.py:185
  192.1 14.2 %collective-permute-done.22.refs_10_ = bf16[2,10,64,128]{3,2,1,0:T(8,128)(2,1)S(1)} collective-permute-done((bf16[2,10,64,128]{3,2,1,0:T(8,128)(2,1)S(1)}, bf16[2,10,64,128]{3,2,1,0:T(8,128)(2,1)S(1)}, u32[]{:S(2)}, u32[]{:S(2)}) %collective-permute-start.22) | collective-permute-done | bytes 327712 | tf_op jit(solution)/shard_map/ppermute | solution.py:297
  206.3 10.5 %collective-permute-done.26.refs_14_ = bf16[2,10,64,128]{3,2,1,0:T(8,128)(2,1)S(1)} collective-permute-done((bf16[2,10,64,128]{3,2,1,0:T(8,128)(2,1)S(1)}, bf16[2,10,64,128]{3,2,1,0:T(8,128)(2,1)S(1)}, u32[]{:S(2)}, u32[]{:S(2)}) %collective-permute-start.26) | collective-permute-done | bytes 327712 | tf_op jit(solution)/shard_map/ppermute | solution.py:297
  216.8 17.8 %collective-permute-start.32 = (bf16[2,16,64,128]{3,2,1,0:T(8,128)(2,1)}, bf16[2,16,64,128]{3,2,1,0:T(8,128)(2,1)S(1)}, u32[]{:S(2)}, u32[]{:S(2)}) collective-permute-start(bf16[2,16,64,128]{3,2,1,0:T(8,128)(2,1)} %get-tuple-element.153), channel_id=1, source_target_pairs={{0,20},{4,16},{8,28},{12,24},{16,4},{20,0},{24,12},{28,8},{1,21},{... | collective-permute-start | bytes 1572872 | tf_op jit(solution)/shard_map/ppermute | solution.py:297
  235.9 17.5 %collective-permute-start.29 = (bf16[2,16,64,128]{3,2,1,0:T(8,128)(2,1)}, bf16[2,16,64,128]{3,2,1,0:T(8,128)(2,1)S(1)}, u32[]{:S(2)}, u32[]{:S(2)}) collective-permute-start(bf16[2,16,64,128]{3,2,1,0:T(8,128)(2,1)} %get-tuple-element.145), channel_id=1, source_target_pairs={{0,8},{4,12},{8,0},{12,4},{16,24},{20,28},{24,16},{28,20},{1,9},{5... | collective-permute-start | bytes 1572872 | tf_op jit(solution)/shard_map/ppermute | solution.py:297
  258.7 6.5 %all-to-all-done.2.block = bf16[4,2,32,128,128]{4,3,2,1,0:T(8,128)(2,1)} async-done(((bf16[4,2,32,128,128]{4,3,2,1,0:T(8,128)(2,1)}), bf16[4,2,32,128,128]{4,3,2,1,0:T(8,128)(2,1)}, u32[]{:S(2)}, u32[]{:S(2)}) %all-to-all-start.2) | async-done | bytes 8388640 | tf_op jit(solution)/shard_map/all_to_all | solution.py:344
  265.1 16.4 %second.7 = (bf16[2,32,16,128]{3,2,1,0:T(8,128)(2,1)}, bf16[2,32,16,128]{3,2,1,0:T(8,128)(2,1)}, bf16[2,32,16,128]{3,2,1,0:T(8,128)(2,1)}, bf16[2,32,16,128]{3,2...) custom-call(s32[2]{0:T(128)} %pad_add_fusion.place, ...), custom_call_target="tpu_custom_call" | custom-call | flops 8589934592 | bytes 18874368 | tf_op jit(solution)/shard_map/second/pallas_call | solution.py:185
  290.1 24.7 %collective-permute-start.51 = (bf16[2,32,16,128]{3,2,1,0:T(8,128)(2,1)}, bf16[2,32,16,128]{3,2,1,0:T(8,128)(2,1)S(1)}, u32[]{:S(2)}, u32[]{:S(2)}) collective-permute-start(bf16[2,32,16,128]{3,2,1,0:T(8,128)(2,1)} %get-tuple-element.196), channel_id=1, source_target_pairs={{0,8},{4,12},{8,0},{12,4},{16,24},{20,28},{24,16},{28,20},{1,9},{5... | collective-permute-start | bytes 786440 | tf_op jit(solution)/shard_map/ppermute | solution.py:297
  321.6 7.0 %collective-permute-done.51.refs_26_ = bf16[2,32,16,128]{3,2,1,0:T(8,128)(2,1)S(1)} collective-permute-done((bf16[2,32,16,128]{3,2,1,0:T(8,128)(2,1)}, bf16[2,32,16,128]{3,2,1,0:T(8,128)(2,1)S(1)}, u32[]{:S(2)}, u32[]{:S(2)}) %collective-permute-start.51) | collective-permute-done | bytes 262176 | tf_op jit(solution)/shard_map/ppermute | solution.py:297
  330.3 6.4 %collective-permute-done.35.refs_29_ = bf16[2,32,16,128]{3,2,1,0:T(8,128)(2,1)S(1)} collective-permute-done((bf16[2,32,16,128]{3,2,1,0:T(8,128)(2,1)}, bf16[2,32,16,128]{3,2,1,0:T(8,128)(2,1)S(1)}, u32[]{:S(2)}, u32[]{:S(2)}) %collective-permute-start.35) | collective-permute-done | bytes 262176 | tf_op jit(solution)/shard_map/ppermute | solution.py:297
  342.0 7.1 %collective-permute-start.58 = (bf16[2,32,16,128]{3,2,1,0:T(8,128)(2,1)}, bf16[2,32,16,128]{3,2,1,0:T(8,128)(2,1)S(1)}, u32[]{:S(2)}, u32[]{:S(2)}) collective-permute-start(bf16[2,32,16,128]{3,2,1,0:T(8,128)(2,1)} %get-tuple-element.209), channel_id=1, source_target_pairs={{0,8},{4,12},{8,0},{12,4},{16,24},{20,28},{24,16},{28,20},{1,9},{5... | collective-permute-start | bytes 786440 | tf_op jit(solution)/shard_map/ppermute | solution.py:297
  351.1 8.1 %collective-permute-done.36.refs_28_ = bf16[2,32,16,128]{3,2,1,0:T(8,128)(2,1)S(1)} collective-permute-done((bf16[2,32,16,128]{3,2,1,0:T(8,128)(2,1)}, bf16[2,32,16,128]{3,2,1,0:T(8,128)(2,1)S(1)}, u32[]{:S(2)}, u32[]{:S(2)}) %collective-permute-start.36) | collective-permute-done | bytes 262176 | tf_op jit(solution)/shard_map/ppermute | solution.py:297
  368.1 12.4 %collective-permute-done.53.refs_27_ = bf16[2,32,16,128]{3,2,1,0:T(8,128)(2,1)S(1)} collective-permute-done((bf16[2,32,16,128]{3,2,1,0:T(8,128)(2,1)}, bf16[2,32,16,128]{3,2,1,0:T(8,128)(2,1)S(1)}, u32[]{:S(2)}, u32[]{:S(2)}) %collective-permute-start.53) | collective-permute-done | bytes 262176 | tf_op jit(solution)/shard_map/ppermute | solution.py:297
  381.9 11.5 %collective-permute-start.38 = (bf16[2,32,16,128]{3,2,1,0:T(8,128)(2,1)}, bf16[2,32,16,128]{3,2,1,0:T(8,128)(2,1)S(1)}, u32[]{:S(2)}, u32[]{:S(2)}) collective-permute-start(bf16[2,32,16,128]{3,2,1,0:T(8,128)(2,1)} %get-tuple-element.167), channel_id=1, source_target_pairs={{0,8},{4,12},{8,0},{12,4},{16,24},{20,28},{24,16},{28,20},{1,9},{5... | collective-permute-start | bytes 786440 | tf_op jit(solution)/shard_map/ppermute | solution.py:297
  393.5 5.8 %collective-permute-start.49 = (bf16[2,32,16,128]{3,2,1,0:T(8,128)(2,1)}, bf16[2,32,16,128]{3,2,1,0:T(8,128)(2,1)S(1)}, u32[]{:S(2)}, u32[]{:S(2)}) collective-permute-start(bf16[2,32,16,128]{3,2,1,0:T(8,128)(2,1)} %get-tuple-element.189), channel_id=1, source_target_pairs={{0,20},{4,16},{8,28},{12,24},{16,4},{20,0},{24,12},{28,8},{1,21},{... | collective-permute-start | bytes 786440 | tf_op jit(solution)/shard_map/ppermute | solution.py:297
  399.3 10.5 %collective-permute-done.41.refs_29_ = bf16[2,32,16,128]{3,2,1,0:T(8,128)(2,1)S(1)} collective-permute-done((bf16[2,32,16,128]{3,2,1,0:T(8,128)(2,1)}, bf16[2,32,16,128]{3,2,1,0:T(8,128)(2,1)S(1)}, u32[]{:S(2)}, u32[]{:S(2)}) %collective-permute-start.41) | collective-permute-done | bytes 262176 | tf_op jit(solution)/shard_map/ppermute | solution.py:297
  409.9 11.4 %third.4.refs_32_ = f32[1024,64,128]{2,1,0:T(8,128)} custom-call(s32[2]{0:T(128)} %pad_add_fusion.place, bf16[1024,1024]{1,0:T(8,128)(2,1)} %maximum_maximum_fusion.mixing, bf16[2,6,64,128]{3,2,1,0:T(8,128)(2,1)} %get-tuple-element.112.refs_0_, bf16[2,6,64,128]{3,2,1,0:T(8,128)(2,1)} %collective-permute-done.14.refs_1_, bf16[2,6,64,128]{3,2,1,0:T(8,128)(2,1)} %copy-done.12, ...), custom_call_target="tpu_custom_call" | custom-call | flops 4294967296 | bytes 14680064 | tf_op jit(solution)/shard_map/third/pallas_call | solution.py:263
  428.5 17.9 %collective-permute-done.42.refs_28_ = bf16[2,32,16,128]{3,2,1,0:T(8,128)(2,1)S(1)} collective-permute-done((bf16[2,32,16,128]{3,2,1,0:T(8,128)(2,1)}, bf16[2,32,16,128]{3,2,1,0:T(8,128)(2,1)S(1)}, u32[]{:S(2)}, u32[]{:S(2)}) %collective-permute-start.42) | collective-permute-done | bytes 262176 | tf_op jit(solution)/shard_map/ppermute | solution.py:297
  448.0 11.7 %third.5.refs_32_ = f32[1024,64,128]{2,1,0:T(8,128)} custom-call(s32[2]{0:T(128)} %pad_add_fusion.place, bf16[1024,1024]{1,0:T(8,128)(2,1)} %maximum_maximum_fusion.mixing, bf16[2,6,64,128]{3,2,1,0:T(8,128)(2,1)} %get-tuple-element.112.refs_0_, bf16[2,6,64,128]{3,2,1,0:T(8,128)(2,1)} %collective-permute-done.14.refs_1_, ...), custom_call_target="tpu_custom_call", output_to_operand_aliasing={{}: (34, {})} | custom-call | flops 4294967296 | bytes 14680064 | tf_op jit(solution)/shard_map/third/pallas_call | solution.py:263
  464.9 10.9 %collective-permute-start.44 = (bf16[2,32,16,128]{3,2,1,0:T(8,128)(2,1)S(1)}, bf16[2,32,16,128]{3,2,1,0:T(8,128)(2,1)S(1)}, u32[]{:S(2)}, u32[]{:S(2)}) collective-permute-start(bf16[2,32,16,128]{3,2,1,0:T(8,128)(2,1)S(1)} %copy-done.51), channel_id=1, source_target_pairs={{0,8},{4,12},{8,0},{12,4},{16,24},{20,28},{24,16},{28,20},{1,9},{5... | collective-permute-start | bytes 786440 | tf_op jit(solution)/shard_map/ppermute | solution.py:297
  475.8 11.4 %third.6.refs_32_ = f32[1024,64,128]{2,1,0:T(8,128)} custom-call(s32[2]{0:T(128)} %pad_add_fusion.place, bf16[1024,1024]{1,0:T(8,128)(2,1)} %maximum_maximum_fusion.mixing, bf16[2,6,64,128]{3,2,1,0:T(8,128)(2,1)} %get-tuple-element.112.refs_0_, bf16[2,6,64,128]{3,2,1,0:T(8,128)(2,1)} %collective-permute-done.14.refs_1_, ...), custom_call_target="tpu_custom_call", output_to_operand_aliasing={{}: (34, {})} | custom-call | flops 4294967296 | bytes 14680064 | tf_op jit(solution)/shard_map/third/pallas_call | solution.py:263
  488.4 11.4 %third.7 = f32[1024,64,128]{2,1,0:T(8,128)} custom-call(s32[2]{0:T(128)} %pad_add_fusion.place, bf16[1024,1024]{1,0:T(8,128)(2,1)} %maximum_maximum_fusion.mixing, bf16[2,6,64,128]{3,2,1,0:T(8,128)(2,1)} %get-tuple-element.112.refs_0_, bf16[2,6,64,128]{3,2,1,0:T(8,128)(2,1)} %collective-permute-done.14.refs_1_, ...), custom_call_target="tpu_custom_call", output_to_operand_aliasing={{}: (34, {})} | custom-call | flops 4294967296 | bytes 14680064 | tf_op jit(solution)/shard_map/third/pallas_call | solution.py:263
  (253 shorter events, 152.7 us)
Async XLA Ops:
  6.5 63.7 %all-gather.3.cloned.1.call-start = ((), (), s32[]{:S(2)}) async-start(), calls=%async_computation.3 | async-start | bytes 7864320 | tf_op jit(solution)/shard_map/all_gather | solution.py:352
  76.8 34.9 %all-to-all-start = ((bf16[4,2,10,128,128]{4,3,2,1,0:T(8,128)(2,1)}), bf16[4,2,10,128,128]{4,3,2,1,0:T(8,128)(2,1)S(1)}, u32[]{:S(2)}, u32[]{:S(2)}) async-start(bf16[4,2,10,128,128]{4,3,2,1,0:T(8,128)(2,1)} %first.3), calls=%async_computation | async-start | bytes 5242880 | tf_op jit(solution)/shard_map/all_to_all | solution.py:344
  113.2 53.1 %all-to-all-start.1 = ((bf16[4,2,16,128,128]{4,3,2,1,0:T(8,128)(2,1)}), bf16[4,2,16,128,128]{4,3,2,1,0:T(8,128)(2,1)}, u32[]{:S(2)}, u32[]{:S(2)}) async-start(bf16[4,2,16,128,128]{4,3,2,1,0:T(8,128)(2,1)} %first.4), calls=%async_computation.1 | async-start | bytes 8388608 | tf_op jit(solution)/shard_map/all_to_all | solution.py:344
  133.6 28.3 %collective-permute-start.24 = (bf16[2,10,64,128]{3,2,1,0:T(8,128)(2,1)}, bf16[2,10,64,128]{3,2,1,0:T(8,128)(2,1)}, u32[]{:S(2)}, u32[]{:S(2)}) collective-permute-start(bf16[2,10,64,128]{3,2,1,0:T(8,128)(2,1)} %get-tuple-element.134), channel_id=1, source_target_pairs={{0,16},{4,20},{8,24},{12,28},{16,0},{20,4},{24,8},{28,12},{1,17},{... | collective-permute-start | bytes 983048 | tf_op jit(solution)/shard_map/ppermute | solution.py:297
  134.8 27.1 %collective-permute-start.21 = (bf16[2,10,64,128]{3,2,1,0:T(8,128)(2,1)}, bf16[2,10,64,128]{3,2,1,0:T(8,128)(2,1)}, u32[]{:S(2)}, u32[]{:S(2)}) collective-permute-start(bf16[2,10,64,128]{3,2,1,0:T(8,128)(2,1)} %get-tuple-element.126), channel_id=1, source_target_pairs={{0,4},{4,0},{8,12},{12,8},{16,20},{20,16},{24,28},{28,24},{1,5},{5... | collective-permute-start | bytes 983048 | tf_op jit(solution)/shard_map/ppermute | solution.py:297
  166.3 98.8 %all-to-all-start.2 = ((bf16[4,2,32,128,128]{4,3,2,1,0:T(8,128)(2,1)}), bf16[4,2,32,128,128]{4,3,2,1,0:T(8,128)(2,1)}, u32[]{:S(2)}, u32[]{:S(2)}) async-start(bf16[4,2,32,128,128]{4,3,2,1,0:T(8,128)(2,1)} %first.5), calls=%async_computation.2 | async-start | bytes 16777216 | tf_op jit(solution)/shard_map/all_to_all | solution.py:344
  185.2 70.7 %collective-permute-start.31 = (bf16[2,16,64,128]{3,2,1,0:T(8,128)(2,1)}, bf16[2,16,64,128]{3,2,1,0:T(8,128)(2,1)S(1)}, u32[]{:S(2)}, u32[]{:S(2)}) collective-permute-start(bf16[2,16,64,128]{3,2,1,0:T(8,128)(2,1)} %get-tuple-element.151), channel_id=1, source_target_pairs={{0,16},{4,20},{8,24},{12,28},{16,0},{20,4},{24,8},{28,12},{1,17},{... | collective-permute-start | bytes 1572872 | tf_op jit(solution)/shard_map/ppermute | solution.py:297
  187.3 29.5 %collective-permute-start.26 = (bf16[2,10,64,128]{3,2,1,0:T(8,128)(2,1)S(1)}, bf16[2,10,64,128]{3,2,1,0:T(8,128)(2,1)S(1)}, u32[]{:S(2)}, u32[]{:S(2)}) collective-permute-start(bf16[2,10,64,128]{3,2,1,0:T(8,128)(2,1)S(1)} %copy-done.49), channel_id=1, source_target_pairs={{0,24},{4,28},{8,16},{12,20},{16,8},{20,12},{24,0},{28,4},{1,25},{... | collective-permute-start | bytes 983048 | tf_op jit(solution)/shard_map/ppermute | solution.py:297
  189.9 45.3 %collective-permute-start.27 = (bf16[2,10,64,128]{3,2,1,0:T(8,128)(2,1)S(1)}, bf16[2,10,64,128]{3,2,1,0:T(8,128)(2,1)S(1)}, u32[]{:S(2)}, u32[]{:S(2)}) collective-permute-start(bf16[2,10,64,128]{3,2,1,0:T(8,128)(2,1)S(1)} %copy-done.48), channel_id=1, source_target_pairs={{0,28},{4,24},{8,20},{12,16},{16,12},{20,8},{24,4},{28,0},{1,29},{... | collective-permute-start | bytes 983048 | tf_op jit(solution)/shard_map/ppermute | solution.py:297
  192.1 61.4 %collective-permute-start.23 = (bf16[2,10,64,128]{3,2,1,0:T(8,128)(2,1)S(1)}, bf16[2,10,64,128]{3,2,1,0:T(8,128)(2,1)S(1)}, u32[]{:S(2)}, u32[]{:S(2)}) collective-permute-start(bf16[2,10,64,128]{3,2,1,0:T(8,128)(2,1)S(1)} %copy-done.47), channel_id=1, source_target_pairs={{0,12},{4,8},{8,4},{12,0},{16,28},{20,24},{24,20},{28,16},{1,13},{... | collective-permute-start | bytes 983048 | tf_op jit(solution)/shard_map/ppermute | solution.py:297
  216.8 66.8 %collective-permute-start.32 = (bf16[2,16,64,128]{3,2,1,0:T(8,128)(2,1)}, bf16[2,16,64,128]{3,2,1,0:T(8,128)(2,1)S(1)}, u32[]{:S(2)}, u32[]{:S(2)}) collective-permute-start(bf16[2,16,64,128]{3,2,1,0:T(8,128)(2,1)} %get-tuple-element.153), channel_id=1, source_target_pairs={{0,20},{4,16},{8,28},{12,24},{16,4},{20,0},{24,12},{28,8},{1,21},{... | collective-permute-start | bytes 1572872 | tf_op jit(solution)/shard_map/ppermute | solution.py:297
  234.6 46.9 %collective-permute-start.28 = (bf16[2,16,64,128]{3,2,1,0:T(8,128)(2,1)}, bf16[2,16,64,128]{3,2,1,0:T(8,128)(2,1)S(1)}, u32[]{:S(2)}, u32[]{:S(2)}) collective-permute-start(bf16[2,16,64,128]{3,2,1,0:T(8,128)(2,1)} %get-tuple-element.143), channel_id=1, source_target_pairs={{0,4},{4,0},{8,12},{12,8},{16,20},{20,16},{24,28},{28,24},{1,5},{5... | collective-permute-start | bytes 1572872 | tf_op jit(solution)/shard_map/ppermute | solution.py:297
  235.9 79.4 %collective-permute-start.29 = (bf16[2,16,64,128]{3,2,1,0:T(8,128)(2,1)}, bf16[2,16,64,128]{3,2,1,0:T(8,128)(2,1)S(1)}, u32[]{:S(2)}, u32[]{:S(2)}) collective-permute-start(bf16[2,16,64,128]{3,2,1,0:T(8,128)(2,1)} %get-tuple-element.145), channel_id=1, source_target_pairs={{0,8},{4,12},{8,0},{12,4},{16,24},{20,28},{24,16},{28,20},{1,9},{5... | collective-permute-start | bytes 1572872 | tf_op jit(solution)/shard_map/ppermute | solution.py:297
  254.2 60.5 %collective-permute-start.33 = (bf16[2,16,64,128]{3,2,1,0:T(8,128)(2,1)}, bf16[2,16,64,128]{3,2,1,0:T(8,128)(2,1)S(1)}, u32[]{:S(2)}, u32[]{:S(2)}) collective-permute-start(bf16[2,16,64,128]{3,2,1,0:T(8,128)(2,1)} %get-tuple-element.155), channel_id=1, source_target_pairs={{0,24},{4,28},{8,16},{12,20},{16,8},{20,12},{24,0},{28,4},{1,25},{... | collective-permute-start | bytes 1572872 | tf_op jit(solution)/shard_map/ppermute | solution.py:297
  255.9 34.2 %collective-permute-start.34 = (bf16[2,16,64,128]{3,2,1,0:T(8,128)(2,1)}, bf16[2,16,64,128]{3,2,1,0:T(8,128)(2,1)S(1)}, u32[]{:S(2)}, u32[]{:S(2)}) collective-permute-start(bf16[2,16,64,128]{3,2,1,0:T(8,128)(2,1)} %get-tuple-element.157), channel_id=1, source_target_pairs={{0,28},{4,24},{8,20},{12,16},{16,12},{20,8},{24,4},{28,0},{1,29},{... | collective-permute-start | bytes 1572872 | tf_op jit(solution)/shard_map/ppermute | solution.py:297
  281.6 57.7 %collective-permute-start.30 = (bf16[2,16,64,128]{3,2,1,0:T(8,128)(2,1)S(1)}, bf16[2,16,64,128]{3,2,1,0:T(8,128)(2,1)S(1)}, u32[]{:S(2)}, u32[]{:S(2)}) collective-permute-start(bf16[2,16,64,128]{3,2,1,0:T(8,128)(2,1)S(1)} %copy-done.46), channel_id=1, source_target_pairs={{0,12},{4,8},{8,4},{12,0},{16,28},{20,24},{24,20},{28,16},{1,13},{... | collective-permute-start | bytes 1572872 | tf_op jit(solution)/shard_map/ppermute | solution.py:297
  283.5 37.5 %collective-permute-start.56 = (bf16[2,32,16,128]{3,2,1,0:T(8,128)(2,1)}, bf16[2,32,16,128]{3,2,1,0:T(8,128)(2,1)S(1)}, u32[]{:S(2)}, u32[]{:S(2)}) collective-permute-start(bf16[2,32,16,128]{3,2,1,0:T(8,128)(2,1)} %get-tuple-element.207), channel_id=1, source_target_pairs={{0,16},{4,20},{8,24},{12,28},{16,0},{20,4},{24,8},{28,12},{1,17},{... | collective-permute-start | bytes 786440 | tf_op jit(solution)/shard_map/ppermute | solution.py:297
  290.1 38.5 %collective-permute-start.51 = (bf16[2,32,16,128]{3,2,1,0:T(8,128)(2,1)}, bf16[2,32,16,128]{3,2,1,0:T(8,128)(2,1)S(1)}, u32[]{:S(2)}, u32[]{:S(2)}) collective-permute-start(bf16[2,32,16,128]{3,2,1,0:T(8,128)(2,1)} %get-tuple-element.196), channel_id=1, source_target_pairs={{0,8},{4,12},{8,0},{12,4},{16,24},{20,28},{24,16},{28,20},{1,9},{5... | collective-permute-start | bytes 786440 | tf_op jit(solution)/shard_map/ppermute | solution.py:297
  349.1 31.3 %collective-permute-start.53 = (bf16[2,32,16,128]{3,2,1,0:T(8,128)(2,1)}, bf16[2,32,16,128]{3,2,1,0:T(8,128)(2,1)S(1)}, u32[]{:S(2)}, u32[]{:S(2)}) collective-permute-start(bf16[2,32,16,128]{3,2,1,0:T(8,128)(2,1)} %get-tuple-element.198), channel_id=1, source_target_pairs={{0,12},{4,8},{8,4},{12,0},{16,28},{20,24},{24,20},{28,16},{1,13},{... | collective-permute-start | bytes 786440 | tf_op jit(solution)/shard_map/ppermute | solution.py:297
  360.9 32.6 %collective-permute-start.48 = (bf16[2,32,16,128]{3,2,1,0:T(8,128)(2,1)}, bf16[2,32,16,128]{3,2,1,0:T(8,128)(2,1)S(1)}, u32[]{:S(2)}, u32[]{:S(2)}) collective-permute-start(bf16[2,32,16,128]{3,2,1,0:T(8,128)(2,1)} %get-tuple-element.188), channel_id=1, source_target_pairs={{0,24},{4,28},{8,16},{12,20},{16,8},{20,12},{24,0},{28,4},{1,25},{... | collective-permute-start | bytes 786440 | tf_op jit(solution)/shard_map/ppermute | solution.py:297
  363.0 46.8 %collective-permute-start.41 = (bf16[2,32,16,128]{3,2,1,0:T(8,128)(2,1)}, bf16[2,32,16,128]{3,2,1,0:T(8,128)(2,1)S(1)}, u32[]{:S(2)}, u32[]{:S(2)}) collective-permute-start(bf16[2,32,16,128]{3,2,1,0:T(8,128)(2,1)} %get-tuple-element.175), channel_id=1, source_target_pairs={{0,20},{4,16},{8,28},{12,24},{16,4},{20,0},{24,12},{28,8},{1,21},{... | collective-permute-start | bytes 786440 | tf_op jit(solution)/shard_map/ppermute | solution.py:297
  365.9 55.5 %collective-permute-start.59 = (bf16[2,32,16,128]{3,2,1,0:T(8,128)(2,1)}, bf16[2,32,16,128]{3,2,1,0:T(8,128)(2,1)S(1)}, u32[]{:S(2)}, u32[]{:S(2)}) collective-permute-start(bf16[2,32,16,128]{3,2,1,0:T(8,128)(2,1)} %get-tuple-element.210), channel_id=1, source_target_pairs={{0,4},{4,0},{8,12},{12,8},{16,20},{20,16},{24,28},{28,24},{1,5},{5... | collective-permute-start | bytes 786440 | tf_op jit(solution)/shard_map/ppermute | solution.py:297
  380.4 43.6 %collective-permute-start.54 = (bf16[2,32,16,128]{3,2,1,0:T(8,128)(2,1)}, bf16[2,32,16,128]{3,2,1,0:T(8,128)(2,1)S(1)}, u32[]{:S(2)}, u32[]{:S(2)}) collective-permute-start(bf16[2,32,16,128]{3,2,1,0:T(8,128)(2,1)} %get-tuple-element.199), channel_id=1, source_target_pairs={{0,24},{4,28},{8,16},{12,20},{16,8},{20,12},{24,0},{28,4},{1,25},{... | collective-permute-start | bytes 786440 | tf_op jit(solution)/shard_map/ppermute | solution.py:297
  381.9 43.5 %collective-permute-start.38 = (bf16[2,32,16,128]{3,2,1,0:T(8,128)(2,1)}, bf16[2,32,16,128]{3,2,1,0:T(8,128)(2,1)S(1)}, u32[]{:S(2)}, u32[]{:S(2)}) collective-permute-start(bf16[2,32,16,128]{3,2,1,0:T(8,128)(2,1)} %get-tuple-element.167), channel_id=1, source_target_pairs={{0,8},{4,12},{8,0},{12,4},{16,24},{20,28},{24,16},{28,20},{1,9},{5... | collective-permute-start | bytes 786440 | tf_op jit(solution)/shard_map/ppermute | solution.py:297
  393.5 33.3 %collective-permute-start.49 = (bf16[2,32,16,128]{3,2,1,0:T(8,128)(2,1)}, bf16[2,32,16,128]{3,2,1,0:T(8,128)(2,1)S(1)}, u32[]{:S(2)}, u32[]{:S(2)}) collective-permute-start(bf16[2,32,16,128]{3,2,1,0:T(8,128)(2,1)} %get-tuple-element.189), channel_id=1, source_target_pairs={{0,20},{4,16},{8,28},{12,24},{16,4},{20,0},{24,12},{28,8},{1,21},{... | collective-permute-start | bytes 786440 | tf_op jit(solution)/shard_map/ppermute | solution.py:297
  409.8 36.5 %collective-permute-start.42 = (bf16[2,32,16,128]{3,2,1,0:T(8,128)(2,1)}, bf16[2,32,16,128]{3,2,1,0:T(8,128)(2,1)S(1)}, u32[]{:S(2)}, u32[]{:S(2)}) collective-permute-start(bf16[2,32,16,128]{3,2,1,0:T(8,128)(2,1)} %get-tuple-element.176), channel_id=1, source_target_pairs={{0,16},{4,20},{8,24},{12,28},{16,0},{20,4},{24,8},{28,12},{1,17},{... | collective-permute-start | bytes 786440 | tf_op jit(solution)/shard_map/ppermute | solution.py:297
  421.5 38.3 %collective-permute-start.60 = (bf16[2,32,16,128]{3,2,1,0:T(8,128)(2,1)}, bf16[2,32,16,128]{3,2,1,0:T(8,128)(2,1)S(1)}, u32[]{:S(2)}, u32[]{:S(2)}) collective-permute-start(bf16[2,32,16,128]{3,2,1,0:T(8,128)(2,1)} %get-tuple-element.211), channel_id=1, source_target_pairs={{0,12},{4,8},{8,4},{12,0},{16,28},{20,24},{24,20},{28,16},{1,13},{... | collective-permute-start | bytes 786440 | tf_op jit(solution)/shard_map/ppermute | solution.py:297
  424.1 63.2 %collective-permute-start.55 = (bf16[2,32,16,128]{3,2,1,0:T(8,128)(2,1)}, bf16[2,32,16,128]{3,2,1,0:T(8,128)(2,1)S(1)}, u32[]{:S(2)}, u32[]{:S(2)}) collective-permute-start(bf16[2,32,16,128]{3,2,1,0:T(8,128)(2,1)} %get-tuple-element.200), channel_id=1, source_target_pairs={{0,20},{4,16},{8,28},{12,24},{16,4},{20,0},{24,12},{28,8},{1,21},{... | collective-permute-start | bytes 786440 | tf_op jit(solution)/shard_map/ppermute | solution.py:297
  425.4 36.6 %collective-permute-start.39 = (bf16[2,32,16,128]{3,2,1,0:T(8,128)(2,1)}, bf16[2,32,16,128]{3,2,1,0:T(8,128)(2,1)S(1)}, u32[]{:S(2)}, u32[]{:S(2)}) collective-permute-start(bf16[2,32,16,128]{3,2,1,0:T(8,128)(2,1)} %get-tuple-element.168), channel_id=1, source_target_pairs={{0,4},{4,0},{8,12},{12,8},{16,20},{20,16},{24,28},{28,24},{1,5},{5... | collective-permute-start | bytes 786440 | tf_op jit(solution)/shard_map/ppermute | solution.py:297
  426.8 36.5 %collective-permute-start.50 = (bf16[2,32,16,128]{3,2,1,0:T(8,128)(2,1)}, bf16[2,32,16,128]{3,2,1,0:T(8,128)(2,1)S(1)}, u32[]{:S(2)}, u32[]{:S(2)}) collective-permute-start(bf16[2,32,16,128]{3,2,1,0:T(8,128)(2,1)} %get-tuple-element.190), channel_id=1, source_target_pairs={{0,16},{4,20},{8,24},{12,28},{16,0},{20,4},{24,8},{28,12},{1,17},{... | collective-permute-start | bytes 786440 | tf_op jit(solution)/shard_map/ppermute | solution.py:297
  459.8 27.5 %collective-permute-start.61 = (bf16[2,32,16,128]{3,2,1,0:T(8,128)(2,1)S(1)}, bf16[2,32,16,128]{3,2,1,0:T(8,128)(2,1)S(1)}, u32[]{:S(2)}, u32[]{:S(2)}) collective-permute-start(bf16[2,32,16,128]{3,2,1,0:T(8,128)(2,1)S(1)} %copy-done.54), channel_id=1, source_target_pairs={{0,24},{4,28},{8,16},{12,20},{16,8},{20,12},{24,0},{28,4},{1,25},{... | collective-permute-start | bytes 786440 | tf_op jit(solution)/shard_map/ppermute | solution.py:297
  462.0 25.3 %collective-permute-start.45 = (bf16[2,32,16,128]{3,2,1,0:T(8,128)(2,1)S(1)}, bf16[2,32,16,128]{3,2,1,0:T(8,128)(2,1)S(1)}, u32[]{:S(2)}, u32[]{:S(2)}) collective-permute-start(bf16[2,32,16,128]{3,2,1,0:T(8,128)(2,1)S(1)} %copy-done.53), channel_id=1, source_target_pairs={{0,12},{4,8},{8,4},{12,0},{16,28},{20,24},{24,20},{28,16},{1,13},{... | collective-permute-start | bytes 786440 | tf_op jit(solution)/shard_map/ppermute | solution.py:297
  (94 other events, 2749.4 us)
Sparse Core Ops, SparseCore 0:
  9.5 60.3 all-gather.2

commit v3 on v2

--- a/solution.py
+++ b/solution.py
@@ -9,7 +9,7 @@
 
 COUNTS = (3, 5, 8, 16)
 DEPTH = 5
-WAIT = 3
+WAIT = 4
 FIRST = 5
 SECOND = 6
 BLOCK = 16
@@ -43,7 +43,7 @@
         half = block.shape[0] // 2
         low = (lax.axis_index("col") & 1) == 0
         block = jnp.where(low, whole[:half], whole[half:])
-    pieces = 3
+    pieces = 4
     rows = block.shape[0]
     cuts = [rows * p // pieces // 16 * 16 for p in range(pieces)] + [rows]
     parts = [block[cuts[p] : cuts[p + 1]] for p in range(pieces)]
@@ -367,6 +367,7 @@
         chunks.append(send_second(now, waits))
         if q + 2 <= last:
             held = [chunks[q][t] for t in order[:WAIT]]
+            held += chunks[q - 1][1:] if q else []
             swapped = send_first(following, swapped, *held)
     for part in parts:
         tails.append(send_second(part, {}))

time: 508 us -> 505 us (level)
  waiting for transfers between devices: 165 us -> 139 us
  starting transfers between devices: 195 us -> 218 us
    ppermute x49, waiting for transfers between devices: 121 us -> 103 us  [send(): result = lax.ppermute(block, self.axis, flip(lax.axis_size(self.axis), bit))]
    ppermute x49, starting transfers between devices: 161 us -> 179 us  [send(): result = lax.ppermute(block, self.axis, flip(lax.axis_size(self.axis), bit))]
    ppermute x13 -> x17, waiting for transfers between devices: 29 us -> 21.2 us  [take_from_owner(): received = lax.ppermute(block, axis, flip(lax.axis_size(axis), bit))]
    ppermute x13 -> x17, starting transfers between devices: 19.4 us -> 24.8 us  [take_from_owner(): received = lax.ppermute(block, axis, flip(lax.axis_size(axis), bit))]
  transfers between devices with their start and end apart: 67 -> 71, of which waited for: 31 -> 26; matrix products, arithmetic and copies ran while one was open for 1% -> 1% of each run, Pallas kernels for 20% -> 21%
where the time goes in v3:
time: 505 us; the launch traced here: 504 us
  starting transfers between devices  218 us (43%)
  waiting for transfers between devices  139 us (28%)
  Pallas kernels  121 us (24%)
  between operations  14.8 us (3%)
  local copies, waits for them, and re-layouts  6.99 us (1%)
    ppermute x49, starting transfers between devices, send(): result = lax.ppermute(block, self.axis, flip(lax.axis_size(self.axis), bit))  179 us
    ppermute x49, waiting for transfers between devices, send(): result = lax.ppermute(block, self.axis, flip(lax.axis_size(self.axis), bit))  103 us
    pallas_call x4, Pallas kernels, contract_third(): pl.pallas_call(functools.partial(third_kernel, row_count, offsets, rows,...  45.9 us
    pallas_call x4, Pallas kernels, contract_second(): pl.pallas_call(functools.partial(second_kernel, row_count, parts), name='...  38.9 us
    pallas_call x3, Pallas kernels, contract_first(): pl.pallas_call(first_kernel, name='first', grid=(count // step,), in_spec...  30.2 us
    ppermute x17, starting transfers between devices, take_from_owner(): received = lax.ppermute(block, axis, flip(lax.axis_size(axis), bit))  24.8 us
    ppermute x17, waiting for transfers between devices, take_from_owner(): received = lax.ppermute(block, axis, flip(lax.axis_size(axis), bit))  21.2 us
    all_to_all x3, starting transfers between devices, send_first(): return lax.all_to_all(after(block, *others), 'col', 0, 0, tiled=True)  14.4 us
  transfers between devices with their start and end apart: 71, of which 26 were waited for; matrix products, arithmetic and copies ran while one was open for 1% of the time, Pallas kernels for 21%

profile of v3, /device:TPU:0, one launch (start us, length us, event | category | flops | bytes accessed | tf_op | source)
XLA Modules:
  0.0 503.9 jit_solution(644266291059340948)
XLA Ops:
  60.7 7.3 %first.3 = bf16[4,2,10,128,128]{4,3,2,1,0:T(8,128)(2,1)} custom-call(bf16[1024,1024]{1,0:T(8,128)(2,1)} %maximum_maximum_fusion.mixing, bf16[2,64,128,512]{3,2,1,0:T(8,128)(2,1)} %elem.3), custom_call_target="tpu_custom_call" | custom-call | flops 2684354560 | bytes 7340032 | tf_op jit(solution)/shard_map/first/pallas_call | solution.py:85
  68.0 6.5 %gathered.1.block = bf16[4,2,6,128,128]{4,3,2,1,0:T(8,128)(2,1)} custom-call(s32[2]{0:T(128)} %pad_add_fusion.place, bf16[1024,1024]{1,0:T(8,128)(2,1)} %maximum_maximum_fusion.mixing, bf16[4,2,6,128,512]{4,3,2,1,0:T(8,128)(2,1)} %bitcast.11), custom_call_target="tpu_custom_call" | custom-call | flops 1610612736 | bytes 5242880 | tf_op jit(solution)/shard_map/gathered/pallas_call | solution.py:126
  78.1 5.7 %second.4 = (bf16[2,6,64,128]{3,2,1,0:T(8,128)(2,1)}, bf16[2,6,64,128]{3,2,1,0:T(8,128)(2,1)}, bf16[2,6,64,128]{3,2,1,0:T(8,128)(2,1)}, bf16[2,6,64,128]{3,2,1,0...) custom-call(s32[2]{0:T(128)} %pad_add_fusion.place, ...), custom_call_target="tpu_custom_call" | custom-call | flops 1610612736 | bytes 5242880 | tf_op jit(solution)/shard_map/second/pallas_call | solution.py:185
  88.8 8.5 %first.4 = bf16[4,2,16,128,128]{4,3,2,1,0:T(8,128)(2,1)} custom-call(bf16[1024,1024]{1,0:T(8,128)(2,1)} %maximum_maximum_fusion.mixing, bf16[2,64,128,512]{3,2,1,0:T(8,128)(2,1)} %elem.3), custom_call_target="tpu_custom_call" | custom-call | flops 4294967296 | bytes 10485760 | tf_op jit(solution)/shard_map/first/pallas_call | solution.py:85
  97.3 6.0 %collective-permute-done.21.refs_4_ = bf16[2,6,64,128]{3,2,1,0:T(8,128)(2,1)} collective-permute-done((bf16[2,6,64,128]{3,2,1,0:T(8,128)(2,1)}, bf16[2,6,64,128]{3,2,1,0:T(8,128)(2,1)}, u32[]{:S(2)}, u32[]{:S(2)}) %collective-permute-start.21) | collective-permute-done | bytes 196640 | tf_op jit(solution)/shard_map/ppermute | solution.py:297
  110.9 4.9 all-to-all-start.1
  120.7 7.6 %second.5 = (bf16[2,10,64,128]{3,2,1,0:T(8,128)(2,1)}, bf16[2,10,64,128]{3,2,1,0:T(8,128)(2,1)}, bf16[2,10,64,128]{3,2,1,0:T(8,128)(2,1)}, bf16[2,10,64,128]{3,2...) custom-call(s32[2]{0:T(128)} %pad_add_fusion.place, ...), custom_call_target="tpu_custom_call" | custom-call | flops 2684354560 | bytes 7340032 | tf_op jit(solution)/shard_map/second/pallas_call | solution.py:185
  128.3 5.2 %collective-permute-start.20 = (bf16[2,6,64,128]{3,2,1,0:T(8,128)(2,1)S(1)}, bf16[2,6,64,128]{3,2,1,0:T(8,128)(2,1)S(1)}, u32[]{:S(2)}, u32[]{:S(2)}) collective-permute-start(bf16[2,6,64,128]{3,2,1,0:T(8,128)(2,1)S(1)} %copy-done.52), channel_id=1, source_target_pairs={{0,12},{4,8},{8,4},{12,0},{16,28},{20,24},{24,20},{28,16},{1,13},{... | collective-permute-start | bytes 589832 | tf_op jit(solution)/shard_map/ppermute | solution.py:297
  139.3 14.4 %first.5 = bf16[4,2,32,128,128]{4,3,2,1,0:T(8,128)(2,1)} custom-call(bf16[1024,1024]{1,0:T(8,128)(2,1)} %maximum_maximum_fusion.mixing, bf16[2,64,128,512]{3,2,1,0:T(8,128)(2,1)} %elem.3), custom_call_target="tpu_custom_call" | custom-call | flops 8589934592 | bytes 18874368 | tf_op jit(solution)/shard_map/first/pallas_call | solution.py:85
  153.7 6.6 %collective-permute-done.29.refs_13_ = bf16[2,10,64,128]{3,2,1,0:T(8,128)(2,1)S(1)} collective-permute-done((bf16[2,10,64,128]{3,2,1,0:T(8,128)(2,1)}, bf16[2,10,64,128]{3,2,1,0:T(8,128)(2,1)S(1)}, u32[]{:S(2)}, u32[]{:S(2)}) %collective-permute-start.29) | collective-permute-done | bytes 327712 | tf_op jit(solution)/shard_map/ppermute | solution.py:297
  164.3 5.8 %all-to-all-start.2 = ((bf16[4,2,32,128,128]{4,3,2,1,0:T(8,128)(2,1)}), bf16[4,2,32,128,128]{4,3,2,1,0:T(8,128)(2,1)}, u32[]{:S(2)}, u32[]{:S(2)}) async-start(bf16[4,2,32,128,128]{4,3,2,1,0:T(8,128)(2,1)} %first.5), calls=%async_computation.2 | async-start | bytes 16777216 | tf_op jit(solution)/shard_map/all_to_all | solution.py:344
  170.1 9.2 %second.6 = (bf16[2,16,64,128]{3,2,1,0:T(8,128)(2,1)}, bf16[2,16,64,128]{3,2,1,0:T(8,128)(2,1)}, bf16[2,16,64,128]{3,2,1,0:T(8,128)(2,1)}, bf16[2,16,64,128]{3,2...) custom-call(s32[2]{0:T(128)} %pad_add_fusion.place, ...), custom_call_target="tpu_custom_call" | custom-call | flops 4294967296 | bytes 10485760 | tf_op jit(solution)/shard_map/second/pallas_call | solution.py:185
  185.4 16.6 %collective-permute-done.30.refs_14_ = bf16[2,10,64,128]{3,2,1,0:T(8,128)(2,1)S(1)} collective-permute-done((bf16[2,10,64,128]{3,2,1,0:T(8,128)(2,1)S(1)}, bf16[2,10,64,128]{3,2,1,0:T(8,128)(2,1)S(1)}, u32[]{:S(2)}, u32[]{:S(2)}) %collective-permute-start.30) | collective-permute-done | bytes 327712 | tf_op jit(solution)/shard_map/ppermute | solution.py:297
  202.0 27.2 %collective-permute-start.36 = (bf16[2,16,64,128]{3,2,1,0:T(8,128)(2,1)}, bf16[2,16,64,128]{3,2,1,0:T(8,128)(2,1)S(1)}, u32[]{:S(2)}, u32[]{:S(2)}) collective-permute-start(bf16[2,16,64,128]{3,2,1,0:T(8,128)(2,1)} %get-tuple-element.153), channel_id=1, source_target_pairs={{0,20},{4,16},{8,28},{12,24},{16,4},{20,0},{24,12},{28,8},{1,21},{... | collective-permute-start | bytes 1572872 | tf_op jit(solution)/shard_map/ppermute | solution.py:297
  230.3 17.5 %collective-permute-start.33 = (bf16[2,16,64,128]{3,2,1,0:T(8,128)(2,1)}, bf16[2,16,64,128]{3,2,1,0:T(8,128)(2,1)S(1)}, u32[]{:S(2)}, u32[]{:S(2)}) collective-permute-start(bf16[2,16,64,128]{3,2,1,0:T(8,128)(2,1)} %get-tuple-element.145), channel_id=1, source_target_pairs={{0,8},{4,12},{8,0},{12,4},{16,24},{20,28},{24,16},{28,20},{1,9},{5... | collective-permute-start | bytes 1572872 | tf_op jit(solution)/shard_map/ppermute | solution.py:297
  251.7 11.4 %all-to-all-done.2.block = bf16[4,2,32,128,128]{4,3,2,1,0:T(8,128)(2,1)} async-done(((bf16[4,2,32,128,128]{4,3,2,1,0:T(8,128)(2,1)}), bf16[4,2,32,128,128]{4,3,2,1,0:T(8,128)(2,1)}, u32[]{:S(2)}, u32[]{:S(2)}) %all-to-all-start.2) | async-done | bytes 8388640 | tf_op jit(solution)/shard_map/all_to_all | solution.py:344
  263.1 16.4 %second.7 = (bf16[2,32,16,128]{3,2,1,0:T(8,128)(2,1)}, bf16[2,32,16,128]{3,2,1,0:T(8,128)(2,1)}, bf16[2,32,16,128]{3,2,1,0:T(8,128)(2,1)}, bf16[2,32,16,128]{3,2...) custom-call(s32[2]{0:T(128)} %pad_add_fusion.place, ...), custom_call_target="tpu_custom_call" | custom-call | flops 8589934592 | bytes 18874368 | tf_op jit(solution)/shard_map/second/pallas_call | solution.py:185
  284.1 26.3 %collective-permute-start.55 = (bf16[2,32,16,128]{3,2,1,0:T(8,128)(2,1)}, bf16[2,32,16,128]{3,2,1,0:T(8,128)(2,1)S(1)}, u32[]{:S(2)}, u32[]{:S(2)}) collective-permute-start(bf16[2,32,16,128]{3,2,1,0:T(8,128)(2,1)} %get-tuple-element.196), channel_id=1, source_target_pairs={{0,8},{4,12},{8,0},{12,4},{16,24},{20,28},{24,16},{28,20},{1,9},{5... | collective-permute-start | bytes 786440 | tf_op jit(solution)/shard_map/ppermute | solution.py:297
  317.2 7.8 %collective-permute-done.55.refs_26_ = bf16[2,32,16,128]{3,2,1,0:T(8,128)(2,1)S(1)} collective-permute-done((bf16[2,32,16,128]{3,2,1,0:T(8,128)(2,1)}, bf16[2,32,16,128]{3,2,1,0:T(8,128)(2,1)S(1)}, u32[]{:S(2)}, u32[]{:S(2)}) %collective-permute-start.55) | collective-permute-done | bytes 262176 | tf_op jit(solution)/shard_map/ppermute | solution.py:297
  327.2 5.8 %collective-permute-done.39.refs_29_ = bf16[2,32,16,128]{3,2,1,0:T(8,128)(2,1)S(1)} collective-permute-done((bf16[2,32,16,128]{3,2,1,0:T(8,128)(2,1)}, bf16[2,32,16,128]{3,2,1,0:T(8,128)(2,1)S(1)}, u32[]{:S(2)}, u32[]{:S(2)}) %collective-permute-start.39) | collective-permute-done | bytes 262176 | tf_op jit(solution)/shard_map/ppermute | solution.py:297
  338.5 6.7 %collective-permute-start.62 = (bf16[2,32,16,128]{3,2,1,0:T(8,128)(2,1)}, bf16[2,32,16,128]{3,2,1,0:T(8,128)(2,1)S(1)}, u32[]{:S(2)}, u32[]{:S(2)}) collective-permute-start(bf16[2,32,16,128]{3,2,1,0:T(8,128)(2,1)} %get-tuple-element.209), channel_id=1, source_target_pairs={{0,8},{4,12},{8,0},{12,4},{16,24},{20,28},{24,16},{28,20},{1,9},{5... | collective-permute-start | bytes 786440 | tf_op jit(solution)/shard_map/ppermute | solution.py:297
  347.4 8.4 %collective-permute-done.40.refs_28_ = bf16[2,32,16,128]{3,2,1,0:T(8,128)(2,1)S(1)} collective-permute-done((bf16[2,32,16,128]{3,2,1,0:T(8,128)(2,1)}, bf16[2,32,16,128]{3,2,1,0:T(8,128)(2,1)S(1)}, u32[]{:S(2)}, u32[]{:S(2)}) %collective-permute-start.40) | collective-permute-done | bytes 262176 | tf_op jit(solution)/shard_map/ppermute | solution.py:297
  364.3 11.9 %collective-permute-done.57.refs_27_ = bf16[2,32,16,128]{3,2,1,0:T(8,128)(2,1)S(1)} collective-permute-done((bf16[2,32,16,128]{3,2,1,0:T(8,128)(2,1)}, bf16[2,32,16,128]{3,2,1,0:T(8,128)(2,1)S(1)}, u32[]{:S(2)}, u32[]{:S(2)}) %collective-permute-start.57) | collective-permute-done | bytes 262176 | tf_op jit(solution)/shard_map/ppermute | solution.py:297
  377.9 12.9 %collective-permute-start.42 = (bf16[2,32,16,128]{3,2,1,0:T(8,128)(2,1)}, bf16[2,32,16,128]{3,2,1,0:T(8,128)(2,1)S(1)}, u32[]{:S(2)}, u32[]{:S(2)}) collective-permute-start(bf16[2,32,16,128]{3,2,1,0:T(8,128)(2,1)} %get-tuple-element.167), channel_id=1, source_target_pairs={{0,8},{4,12},{8,0},{12,4},{16,24},{20,28},{24,16},{28,20},{1,9},{5... | collective-permute-start | bytes 786440 | tf_op jit(solution)/shard_map/ppermute | solution.py:297
  390.8 5.7 %collective-permute-start.53 = (bf16[2,32,16,128]{3,2,1,0:T(8,128)(2,1)}, bf16[2,32,16,128]{3,2,1,0:T(8,128)(2,1)S(1)}, u32[]{:S(2)}, u32[]{:S(2)}) collective-permute-start(bf16[2,32,16,128]{3,2,1,0:T(8,128)(2,1)} %get-tuple-element.189), channel_id=1, source_target_pairs={{0,20},{4,16},{8,28},{12,24},{16,4},{20,0},{24,12},{28,8},{1,21},{... | collective-permute-start | bytes 786440 | tf_op jit(solution)/shard_map/ppermute | solution.py:297
  396.5 10.6 %collective-permute-done.45.refs_29_ = bf16[2,32,16,128]{3,2,1,0:T(8,128)(2,1)S(1)} collective-permute-done((bf16[2,32,16,128]{3,2,1,0:T(8,128)(2,1)}, bf16[2,32,16,128]{3,2,1,0:T(8,128)(2,1)S(1)}, u32[]{:S(2)}, u32[]{:S(2)}) %collective-permute-start.45) | collective-permute-done | bytes 262176 | tf_op jit(solution)/shard_map/ppermute | solution.py:297
  407.3 11.4 %third.4.refs_32_ = f32[1024,64,128]{2,1,0:T(8,128)} custom-call(s32[2]{0:T(128)} %pad_add_fusion.place, bf16[1024,1024]{1,0:T(8,128)(2,1)} %maximum_maximum_fusion.mixing, bf16[2,6,64,128]{3,2,1,0:T(8,128)(2,1)} %get-tuple-element.112.refs_0_, bf16[2,6,64,128]{3,2,1,0:T(8,128)(2,1)} %collective-permute-done.18.refs_1_, ...), custom_call_target="tpu_custom_call" | custom-call | flops 4294967296 | bytes 14680064 | tf_op jit(solution)/shard_map/third/pallas_call | solution.py:263
  426.3 16.8 %collective-permute-done.46.refs_28_ = bf16[2,32,16,128]{3,2,1,0:T(8,128)(2,1)S(1)} collective-permute-done((bf16[2,32,16,128]{3,2,1,0:T(8,128)(2,1)}, bf16[2,32,16,128]{3,2,1,0:T(8,128)(2,1)S(1)}, u32[]{:S(2)}, u32[]{:S(2)}) %collective-permute-start.46) | collective-permute-done | bytes 262176 | tf_op jit(solution)/shard_map/ppermute | solution.py:297
  445.3 11.7 %third.5.refs_32_ = f32[1024,64,128]{2,1,0:T(8,128)} custom-call(s32[2]{0:T(128)} %pad_add_fusion.place, bf16[1024,1024]{1,0:T(8,128)(2,1)} %maximum_maximum_fusion.mixing, bf16[2,6,64,128]{3,2,1,0:T(8,128)(2,1)} %get-tuple-element.112.refs_0_, bf16[2,6,64,128]{3,2,1,0:T(8,128)(2,1)} %collective-permute-done.18.refs_1_, ...), custom_call_target="tpu_custom_call", output_to_operand_aliasing={{}: (34, {})} | custom-call | flops 4294967296 | bytes 14680064 | tf_op jit(solution)/shard_map/third/pallas_call | solution.py:263
  462.2 10.9 %collective-permute-start.48 = (bf16[2,32,16,128]{3,2,1,0:T(8,128)(2,1)S(1)}, bf16[2,32,16,128]{3,2,1,0:T(8,128)(2,1)S(1)}, u32[]{:S(2)}, u32[]{:S(2)}) collective-permute-start(bf16[2,32,16,128]{3,2,1,0:T(8,128)(2,1)S(1)} %copy-done.48), channel_id=1, source_target_pairs={{0,8},{4,12},{8,0},{12,4},{16,24},{20,28},{24,16},{28,20},{1,9},{5... | collective-permute-start | bytes 786440 | tf_op jit(solution)/shard_map/ppermute | solution.py:297
  473.1 11.4 %third.6.refs_32_ = f32[1024,64,128]{2,1,0:T(8,128)} custom-call(s32[2]{0:T(128)} %pad_add_fusion.place, bf16[1024,1024]{1,0:T(8,128)(2,1)} %maximum_maximum_fusion.mixing, bf16[2,6,64,128]{3,2,1,0:T(8,128)(2,1)} %get-tuple-element.112.refs_0_, bf16[2,6,64,128]{3,2,1,0:T(8,128)(2,1)} %collective-permute-done.18.refs_1_, ...), custom_call_target="tpu_custom_call", output_to_operand_aliasing={{}: (34, {})} | custom-call | flops 4294967296 | bytes 14680064 | tf_op jit(solution)/shard_map/third/pallas_call | solution.py:263
  485.7 11.4 %third.7 = f32[1024,64,128]{2,1,0:T(8,128)} custom-call(s32[2]{0:T(128)} %pad_add_fusion.place, bf16[1024,1024]{1,0:T(8,128)(2,1)} %maximum_maximum_fusion.mixing, bf16[2,6,64,128]{3,2,1,0:T(8,128)(2,1)} %get-tuple-element.112.refs_0_, bf16[2,6,64,128]{3,2,1,0:T(8,128)(2,1)} %collective-permute-done.18.refs_1_, ...), custom_call_target="tpu_custom_call", output_to_operand_aliasing={{}: (34, {})} | custom-call | flops 4294967296 | bytes 14680064 | tf_op jit(solution)/shard_map/third/pallas_call | solution.py:263
  (254 shorter events, 142.6 us)
Async XLA Ops:
  6.5 61.4 %all-gather.3.cloned.1.call-start = ((), (), s32[]{:S(2)}) async-start(), calls=%async_computation.3 | async-start | bytes 7864320 | tf_op jit(solution)/shard_map/all_gather | solution.py:352
  74.5 34.9 %all-to-all-start = ((bf16[4,2,10,128,128]{4,3,2,1,0:T(8,128)(2,1)}), bf16[4,2,10,128,128]{4,3,2,1,0:T(8,128)(2,1)S(1)}, u32[]{:S(2)}, u32[]{:S(2)}) async-start(bf16[4,2,10,128,128]{4,3,2,1,0:T(8,128)(2,1)} %first.3), calls=%async_computation | async-start | bytes 5242880 | tf_op jit(solution)/shard_map/all_to_all | solution.py:344
  110.9 53.4 %all-to-all-start.1 = ((bf16[4,2,16,128,128]{4,3,2,1,0:T(8,128)(2,1)}), bf16[4,2,16,128,128]{4,3,2,1,0:T(8,128)(2,1)}, u32[]{:S(2)}, u32[]{:S(2)}) async-start(bf16[4,2,16,128,128]{4,3,2,1,0:T(8,128)(2,1)} %first.4), calls=%async_computation.1 | async-start | bytes 8388608 | tf_op jit(solution)/shard_map/all_to_all | solution.py:344
  133.5 26.7 %collective-permute-start.29 = (bf16[2,10,64,128]{3,2,1,0:T(8,128)(2,1)}, bf16[2,10,64,128]{3,2,1,0:T(8,128)(2,1)S(1)}, u32[]{:S(2)}, u32[]{:S(2)}) collective-permute-start(bf16[2,10,64,128]{3,2,1,0:T(8,128)(2,1)} %get-tuple-element.136), channel_id=1, source_target_pairs={{0,20},{4,16},{8,28},{12,24},{16,4},{20,0},{24,12},{28,8},{1,21},{... | collective-permute-start | bytes 983048 | tf_op jit(solution)/shard_map/ppermute | solution.py:297
  134.6 29.6 %collective-permute-start.28 = (bf16[2,10,64,128]{3,2,1,0:T(8,128)(2,1)}, bf16[2,10,64,128]{3,2,1,0:T(8,128)(2,1)}, u32[]{:S(2)}, u32[]{:S(2)}) collective-permute-start(bf16[2,10,64,128]{3,2,1,0:T(8,128)(2,1)} %get-tuple-element.134), channel_id=1, source_target_pairs={{0,16},{4,20},{8,24},{12,28},{16,0},{20,4},{24,8},{28,12},{1,17},{... | collective-permute-start | bytes 983048 | tf_op jit(solution)/shard_map/ppermute | solution.py:297
  136.4 27.9 %collective-permute-start.25 = (bf16[2,10,64,128]{3,2,1,0:T(8,128)(2,1)}, bf16[2,10,64,128]{3,2,1,0:T(8,128)(2,1)}, u32[]{:S(2)}, u32[]{:S(2)}) collective-permute-start(bf16[2,10,64,128]{3,2,1,0:T(8,128)(2,1)} %get-tuple-element.126), channel_id=1, source_target_pairs={{0,4},{4,0},{8,12},{12,8},{16,20},{20,16},{24,28},{28,24},{1,5},{5... | collective-permute-start | bytes 983048 | tf_op jit(solution)/shard_map/ppermute | solution.py:297
  137.9 26.3 %collective-permute-start.26 = (bf16[2,10,64,128]{3,2,1,0:T(8,128)(2,1)}, bf16[2,10,64,128]{3,2,1,0:T(8,128)(2,1)}, u32[]{:S(2)}, u32[]{:S(2)}) collective-permute-start(bf16[2,10,64,128]{3,2,1,0:T(8,128)(2,1)} %get-tuple-element.128), channel_id=1, source_target_pairs={{0,8},{4,12},{8,0},{12,4},{16,24},{20,28},{24,16},{28,20},{1,9},{5... | collective-permute-start | bytes 983048 | tf_op jit(solution)/shard_map/ppermute | solution.py:297
  164.3 98.8 %all-to-all-start.2 = ((bf16[4,2,32,128,128]{4,3,2,1,0:T(8,128)(2,1)}), bf16[4,2,32,128,128]{4,3,2,1,0:T(8,128)(2,1)}, u32[]{:S(2)}, u32[]{:S(2)}) async-start(bf16[4,2,32,128,128]{4,3,2,1,0:T(8,128)(2,1)} %first.5), calls=%async_computation.2 | async-start | bytes 16777216 | tf_op jit(solution)/shard_map/all_to_all | solution.py:344
  179.3 71.1 %collective-permute-start.35 = (bf16[2,16,64,128]{3,2,1,0:T(8,128)(2,1)}, bf16[2,16,64,128]{3,2,1,0:T(8,128)(2,1)S(1)}, u32[]{:S(2)}, u32[]{:S(2)}) collective-permute-start(bf16[2,16,64,128]{3,2,1,0:T(8,128)(2,1)} %get-tuple-element.151), channel_id=1, source_target_pairs={{0,16},{4,20},{8,24},{12,28},{16,0},{20,4},{24,8},{28,12},{1,17},{... | collective-permute-start | bytes 1572872 | tf_op jit(solution)/shard_map/ppermute | solution.py:297
  182.0 47.6 %collective-permute-start.31 = (bf16[2,10,64,128]{3,2,1,0:T(8,128)(2,1)S(1)}, bf16[2,10,64,128]{3,2,1,0:T(8,128)(2,1)S(1)}, u32[]{:S(2)}, u32[]{:S(2)}) collective-permute-start(bf16[2,10,64,128]{3,2,1,0:T(8,128)(2,1)S(1)} %copy-done.46), channel_id=1, source_target_pairs={{0,28},{4,24},{8,20},{12,16},{16,12},{20,8},{24,4},{28,0},{1,29},{... | collective-permute-start | bytes 983048 | tf_op jit(solution)/shard_map/ppermute | solution.py:297
  185.4 62.3 %collective-permute-start.27 = (bf16[2,10,64,128]{3,2,1,0:T(8,128)(2,1)S(1)}, bf16[2,10,64,128]{3,2,1,0:T(8,128)(2,1)S(1)}, u32[]{:S(2)}, u32[]{:S(2)}) collective-permute-start(bf16[2,10,64,128]{3,2,1,0:T(8,128)(2,1)S(1)} %copy-done.45), channel_id=1, source_target_pairs={{0,12},{4,8},{8,4},{12,0},{16,28},{20,24},{24,20},{28,16},{1,13},{... | collective-permute-start | bytes 983048 | tf_op jit(solution)/shard_map/ppermute | solution.py:297
  202.0 78.8 %collective-permute-start.36 = (bf16[2,16,64,128]{3,2,1,0:T(8,128)(2,1)}, bf16[2,16,64,128]{3,2,1,0:T(8,128)(2,1)S(1)}, u32[]{:S(2)}, u32[]{:S(2)}) collective-permute-start(bf16[2,16,64,128]{3,2,1,0:T(8,128)(2,1)} %get-tuple-element.153), channel_id=1, source_target_pairs={{0,20},{4,16},{8,28},{12,24},{16,4},{20,0},{24,12},{28,8},{1,21},{... | collective-permute-start | bytes 1572872 | tf_op jit(solution)/shard_map/ppermute | solution.py:297
  229.2 50.3 %collective-permute-start.32 = (bf16[2,16,64,128]{3,2,1,0:T(8,128)(2,1)}, bf16[2,16,64,128]{3,2,1,0:T(8,128)(2,1)S(1)}, u32[]{:S(2)}, u32[]{:S(2)}) collective-permute-start(bf16[2,16,64,128]{3,2,1,0:T(8,128)(2,1)} %get-tuple-element.143), channel_id=1, source_target_pairs={{0,4},{4,0},{8,12},{12,8},{16,20},{20,16},{24,28},{28,24},{1,5},{5... | collective-permute-start | bytes 1572872 | tf_op jit(solution)/shard_map/ppermute | solution.py:297
  230.3 82.1 %collective-permute-start.33 = (bf16[2,16,64,128]{3,2,1,0:T(8,128)(2,1)}, bf16[2,16,64,128]{3,2,1,0:T(8,128)(2,1)S(1)}, u32[]{:S(2)}, u32[]{:S(2)}) collective-permute-start(bf16[2,16,64,128]{3,2,1,0:T(8,128)(2,1)} %get-tuple-element.145), channel_id=1, source_target_pairs={{0,8},{4,12},{8,0},{12,4},{16,24},{20,28},{24,16},{28,20},{1,9},{5... | collective-permute-start | bytes 1572872 | tf_op jit(solution)/shard_map/ppermute | solution.py:297
  248.5 61.9 %collective-permute-start.37 = (bf16[2,16,64,128]{3,2,1,0:T(8,128)(2,1)}, bf16[2,16,64,128]{3,2,1,0:T(8,128)(2,1)S(1)}, u32[]{:S(2)}, u32[]{:S(2)}) collective-permute-start(bf16[2,16,64,128]{3,2,1,0:T(8,128)(2,1)} %get-tuple-element.155), channel_id=1, source_target_pairs={{0,24},{4,28},{8,16},{12,20},{16,8},{20,12},{24,0},{28,4},{1,25},{... | collective-permute-start | bytes 1572872 | tf_op jit(solution)/shard_map/ppermute | solution.py:297
  250.4 33.7 %collective-permute-start.38 = (bf16[2,16,64,128]{3,2,1,0:T(8,128)(2,1)}, bf16[2,16,64,128]{3,2,1,0:T(8,128)(2,1)S(1)}, u32[]{:S(2)}, u32[]{:S(2)}) collective-permute-start(bf16[2,16,64,128]{3,2,1,0:T(8,128)(2,1)} %get-tuple-element.157), channel_id=1, source_target_pairs={{0,28},{4,24},{8,20},{12,16},{16,12},{20,8},{24,4},{28,0},{1,29},{... | collective-permute-start | bytes 1572872 | tf_op jit(solution)/shard_map/ppermute | solution.py:297
  279.5 57.3 %collective-permute-start.34 = (bf16[2,16,64,128]{3,2,1,0:T(8,128)(2,1)S(1)}, bf16[2,16,64,128]{3,2,1,0:T(8,128)(2,1)S(1)}, u32[]{:S(2)}, u32[]{:S(2)}) collective-permute-start(bf16[2,16,64,128]{3,2,1,0:T(8,128)(2,1)S(1)} %copy-done.44), channel_id=1, source_target_pairs={{0,12},{4,8},{8,4},{12,0},{16,28},{20,24},{24,20},{28,16},{1,13},{... | collective-permute-start | bytes 1572872 | tf_op jit(solution)/shard_map/ppermute | solution.py:297
  280.8 35.1 %collective-permute-start.60 = (bf16[2,32,16,128]{3,2,1,0:T(8,128)(2,1)}, bf16[2,32,16,128]{3,2,1,0:T(8,128)(2,1)S(1)}, u32[]{:S(2)}, u32[]{:S(2)}) collective-permute-start(bf16[2,32,16,128]{3,2,1,0:T(8,128)(2,1)} %get-tuple-element.207), channel_id=1, source_target_pairs={{0,16},{4,20},{8,24},{12,28},{16,0},{20,4},{24,8},{28,12},{1,17},{... | collective-permute-start | bytes 786440 | tf_op jit(solution)/shard_map/ppermute | solution.py:297
  284.1 41.0 %collective-permute-start.55 = (bf16[2,32,16,128]{3,2,1,0:T(8,128)(2,1)}, bf16[2,32,16,128]{3,2,1,0:T(8,128)(2,1)S(1)}, u32[]{:S(2)}, u32[]{:S(2)}) collective-permute-start(bf16[2,32,16,128]{3,2,1,0:T(8,128)(2,1)} %get-tuple-element.196), channel_id=1, source_target_pairs={{0,8},{4,12},{8,0},{12,4},{16,24},{20,28},{24,16},{28,20},{1,9},{5... | collective-permute-start | bytes 786440 | tf_op jit(solution)/shard_map/ppermute | solution.py:297
  345.3 31.0 %collective-permute-start.57 = (bf16[2,32,16,128]{3,2,1,0:T(8,128)(2,1)}, bf16[2,32,16,128]{3,2,1,0:T(8,128)(2,1)S(1)}, u32[]{:S(2)}, u32[]{:S(2)}) collective-permute-start(bf16[2,32,16,128]{3,2,1,0:T(8,128)(2,1)} %get-tuple-element.198), channel_id=1, source_target_pairs={{0,12},{4,8},{8,4},{12,0},{16,28},{20,24},{24,20},{28,16},{1,13},{... | collective-permute-start | bytes 786440 | tf_op jit(solution)/shard_map/ppermute | solution.py:297
  357.2 33.6 %collective-permute-start.52 = (bf16[2,32,16,128]{3,2,1,0:T(8,128)(2,1)}, bf16[2,32,16,128]{3,2,1,0:T(8,128)(2,1)S(1)}, u32[]{:S(2)}, u32[]{:S(2)}) collective-permute-start(bf16[2,32,16,128]{3,2,1,0:T(8,128)(2,1)} %get-tuple-element.188), channel_id=1, source_target_pairs={{0,24},{4,28},{8,16},{12,20},{16,8},{20,12},{24,0},{28,4},{1,25},{... | collective-permute-start | bytes 786440 | tf_op jit(solution)/shard_map/ppermute | solution.py:297
  359.4 47.8 %collective-permute-start.45 = (bf16[2,32,16,128]{3,2,1,0:T(8,128)(2,1)}, bf16[2,32,16,128]{3,2,1,0:T(8,128)(2,1)S(1)}, u32[]{:S(2)}, u32[]{:S(2)}) collective-permute-start(bf16[2,32,16,128]{3,2,1,0:T(8,128)(2,1)} %get-tuple-element.175), channel_id=1, source_target_pairs={{0,20},{4,16},{8,28},{12,24},{16,4},{20,0},{24,12},{28,8},{1,21},{... | collective-permute-start | bytes 786440 | tf_op jit(solution)/shard_map/ppermute | solution.py:297
  361.9 56.8 %collective-permute-start.63 = (bf16[2,32,16,128]{3,2,1,0:T(8,128)(2,1)}, bf16[2,32,16,128]{3,2,1,0:T(8,128)(2,1)S(1)}, u32[]{:S(2)}, u32[]{:S(2)}) collective-permute-start(bf16[2,32,16,128]{3,2,1,0:T(8,128)(2,1)} %get-tuple-element.210), channel_id=1, source_target_pairs={{0,4},{4,0},{8,12},{12,8},{16,20},{20,16},{24,28},{28,24},{1,5},{5... | collective-permute-start | bytes 786440 | tf_op jit(solution)/shard_map/ppermute | solution.py:297
  376.3 45.6 %collective-permute-start.58 = (bf16[2,32,16,128]{3,2,1,0:T(8,128)(2,1)}, bf16[2,32,16,128]{3,2,1,0:T(8,128)(2,1)S(1)}, u32[]{:S(2)}, u32[]{:S(2)}) collective-permute-start(bf16[2,32,16,128]{3,2,1,0:T(8,128)(2,1)} %get-tuple-element.199), channel_id=1, source_target_pairs={{0,24},{4,28},{8,16},{12,20},{16,8},{20,12},{24,0},{28,4},{1,25},{... | collective-permute-start | bytes 786440 | tf_op jit(solution)/shard_map/ppermute | solution.py:297
  377.9 44.2 %collective-permute-start.42 = (bf16[2,32,16,128]{3,2,1,0:T(8,128)(2,1)}, bf16[2,32,16,128]{3,2,1,0:T(8,128)(2,1)S(1)}, u32[]{:S(2)}, u32[]{:S(2)}) collective-permute-start(bf16[2,32,16,128]{3,2,1,0:T(8,128)(2,1)} %get-tuple-element.167), channel_id=1, source_target_pairs={{0,8},{4,12},{8,0},{12,4},{16,24},{20,28},{24,16},{28,20},{1,9},{5... | collective-permute-start | bytes 786440 | tf_op jit(solution)/shard_map/ppermute | solution.py:297
  390.8 33.3 %collective-permute-start.53 = (bf16[2,32,16,128]{3,2,1,0:T(8,128)(2,1)}, bf16[2,32,16,128]{3,2,1,0:T(8,128)(2,1)S(1)}, u32[]{:S(2)}, u32[]{:S(2)}) collective-permute-start(bf16[2,32,16,128]{3,2,1,0:T(8,128)(2,1)} %get-tuple-element.189), channel_id=1, source_target_pairs={{0,20},{4,16},{8,28},{12,24},{16,4},{20,0},{24,12},{28,8},{1,21},{... | collective-permute-start | bytes 786440 | tf_op jit(solution)/shard_map/ppermute | solution.py:297
  407.1 35.9 %collective-permute-start.46 = (bf16[2,32,16,128]{3,2,1,0:T(8,128)(2,1)}, bf16[2,32,16,128]{3,2,1,0:T(8,128)(2,1)S(1)}, u32[]{:S(2)}, u32[]{:S(2)}) collective-permute-start(bf16[2,32,16,128]{3,2,1,0:T(8,128)(2,1)} %get-tuple-element.176), channel_id=1, source_target_pairs={{0,16},{4,20},{8,24},{12,28},{16,0},{20,4},{24,8},{28,12},{1,17},{... | collective-permute-start | bytes 786440 | tf_op jit(solution)/shard_map/ppermute | solution.py:297
  418.8 38.2 %collective-permute-start.64 = (bf16[2,32,16,128]{3,2,1,0:T(8,128)(2,1)}, bf16[2,32,16,128]{3,2,1,0:T(8,128)(2,1)S(1)}, u32[]{:S(2)}, u32[]{:S(2)}) collective-permute-start(bf16[2,32,16,128]{3,2,1,0:T(8,128)(2,1)} %get-tuple-element.211), channel_id=1, source_target_pairs={{0,12},{4,8},{8,4},{12,0},{16,28},{20,24},{24,20},{28,16},{1,13},{... | collective-permute-start | bytes 786440 | tf_op jit(solution)/shard_map/ppermute | solution.py:297
  421.9 62.7 %collective-permute-start.59 = (bf16[2,32,16,128]{3,2,1,0:T(8,128)(2,1)}, bf16[2,32,16,128]{3,2,1,0:T(8,128)(2,1)S(1)}, u32[]{:S(2)}, u32[]{:S(2)}) collective-permute-start(bf16[2,32,16,128]{3,2,1,0:T(8,128)(2,1)} %get-tuple-element.200), channel_id=1, source_target_pairs={{0,20},{4,16},{8,28},{12,24},{16,4},{20,0},{24,12},{28,8},{1,21},{... | collective-permute-start | bytes 786440 | tf_op jit(solution)/shard_map/ppermute | solution.py:297
  422.1 37.2 %collective-permute-start.43 = (bf16[2,32,16,128]{3,2,1,0:T(8,128)(2,1)}, bf16[2,32,16,128]{3,2,1,0:T(8,128)(2,1)S(1)}, u32[]{:S(2)}, u32[]{:S(2)}) collective-permute-start(bf16[2,32,16,128]{3,2,1,0:T(8,128)(2,1)} %get-tuple-element.168), channel_id=1, source_target_pairs={{0,4},{4,0},{8,12},{12,8},{16,20},{20,16},{24,28},{28,24},{1,5},{5... | collective-permute-start | bytes 786440 | tf_op jit(solution)/shard_map/ppermute | solution.py:297
  424.1 35.8 %collective-permute-start.54 = (bf16[2,32,16,128]{3,2,1,0:T(8,128)(2,1)}, bf16[2,32,16,128]{3,2,1,0:T(8,128)(2,1)S(1)}, u32[]{:S(2)}, u32[]{:S(2)}) collective-permute-start(bf16[2,32,16,128]{3,2,1,0:T(8,128)(2,1)} %get-tuple-element.190), channel_id=1, source_target_pairs={{0,16},{4,20},{8,24},{12,28},{16,0},{20,4},{24,8},{28,12},{1,17},{... | collective-permute-start | bytes 786440 | tf_op jit(solution)/shard_map/ppermute | solution.py:297
  457.1 27.5 %collective-permute-start.65 = (bf16[2,32,16,128]{3,2,1,0:T(8,128)(2,1)S(1)}, bf16[2,32,16,128]{3,2,1,0:T(8,128)(2,1)S(1)}, u32[]{:S(2)}, u32[]{:S(2)}) collective-permute-start(bf16[2,32,16,128]{3,2,1,0:T(8,128)(2,1)S(1)} %copy-done.51), channel_id=1, source_target_pairs={{0,24},{4,28},{8,16},{12,20},{16,8},{20,12},{24,0},{28,4},{1,25},{... | collective-permute-start | bytes 786440 | tf_op jit(solution)/shard_map/ppermute | solution.py:297
  (94 other events, 2571.7 us)
Sparse Core Ops, SparseCore 0:
  9.5 57.4 all-gather.2
